TPU v7x, 128 devices: a whole 4x4x4 slice. The times are simulated.
128 devices in a mesh: ctx: 64 (over x, z_lo, y, core), head: 2 (over z_hi).
Axes of the slice: x: 4, y: 4, z: 4 (z_hi: 2, z_lo: 2; z = z_hi * 2 + z_lo), core: 2. Of those that a mesh axis runs over, the one named last changes fastest.
Arguments:
- img_q: bfloat16 [2048, 1536], P('ctx', 'head'), may hold values from -12 to 12
- img_k: bfloat16 [2048, 1536], P('ctx', 'head'), may hold values from -12 to 12
- img_v: bfloat16 [2048, 1536], P('ctx', 'head'), may hold values from -6 to 6
- txt_ids: int32 [512], replicated, may hold values from 0 to 32767
- concept_ids: int32 [1024], replicated, may hold values from 0 to 32767
- step_index: int32 [1], replicated, may hold values from 0 to 27
- token_table: bfloat16 [32768, 3072], P(('ctx', 'head')), may hold values from -6 to 6
- modulation: float32 [28, 2, 3072], replicated, may hold values from -3 to 3
- txt_qkv: bfloat16 [3072, 3, 1536], P(None, None, 'head'), may hold values from -0.109375 to 0.109375
- qk_gain: float32 [2, 128], replicated, may hold values from 0.25 to 1.75
Outputs:
- img_out: bfloat16 [2048, 1536], P('ctx', 'head')
- saliency: float32 [1024, 2048], P(None, 'ctx')
All inputs are finite; a program needn't handle non-finite values.
Results may differ from a plain program's by a relative error of at most 0.013.
Values may be sent and summed in bfloat16 or wider, within the bound.
No kernel may reach another device: no remote copies, remote signals or barrier semaphores. Data moves between devices by JAX's collectives and lax.ppermute only.
A program may use at most 128 MiB of HBM per device.

v0:
```python
import jax
import jax.numpy as jnp
from jax import lax
from jax.sharding import PartitionSpec as P


def modulate(rows, shift_scale):
    values = rows.astype(jnp.float32)
    mean = jnp.mean(values, axis=1, keepdims=True)
    centered = values - mean
    var = jnp.mean(centered * centered, axis=1, keepdims=True)
    normed = centered * lax.rsqrt(var + 1e-06)
    return (normed * (1.0 + shift_scale[1]) + shift_scale[0]).astype(jnp.bfloat16)


def head_norm(values, gain, head_dim):
    shaped = values.reshape(values.shape[0], -1, head_dim)
    meansq = jnp.mean(shaped * shaped, axis=2, keepdims=True)
    return (shaped * lax.rsqrt(meansq + 1e-06) * gain).reshape(values.shape[0], -1)


def block_stats(queries, keys, values):
    scores = jnp.einsum(
        "rgd,kgd->grk", queries, keys, preferred_element_type=jnp.float32
    ) * queries.shape[-1] ** (-0.5)
    peak = jnp.max(scores, axis=2)
    weights = jnp.exp(scores - peak[:, :, None])
    total = jnp.sum(weights, axis=2)
    summed = jnp.einsum(
        "grk,kgd->grd", weights.astype(jnp.bfloat16), values, preferred_element_type=jnp.float32
    )
    return (peak, total, summed)


def combine_stats(first, second):
    peak = jnp.maximum(first[0], second[0])
    left = jnp.exp(first[0] - peak)
    right = jnp.exp(second[0] - peak)
    total = first[1] * left + second[1] * right
    summed = first[2] * left[:, :, None] + second[2] * right[:, :, None]
    return (peak, total, summed)


def scaled_scores(dots, concept_sq, image_sq, width):
    concept_rms = jnp.sqrt(concept_sq / width + 1e-06)
    image_rms = jnp.sqrt(image_sq / width + 1e-06)
    return dots / (jnp.sqrt(jnp.float32(width)) * concept_rms[:, None] * image_rms[None, :])


def on_device(
    img_q, img_k, img_v, txt_ids, concept_ids, step_index, token_table, modulation, txt_qkv, qk_gain
):
    n_ctx = lax.axis_size("ctx")
    n_head = lax.axis_size("head")
    head_dim = qk_gain.shape[1]
    group = img_q.shape[1] // head_dim
    text_dev = txt_ids.shape[0] // n_ctx
    concept_dev = concept_ids.shape[0] // n_ctx
    vocab_dev = token_table.shape[0]
    combined = jnp.concatenate(
        [txt_ids.reshape(n_ctx, text_dev), concept_ids.reshape(n_ctx, concept_dev)], axis=1
    ).reshape(-1)
    offset = lax.axis_index(("ctx", "head")) * vocab_dev
    wanted = combined - offset
    inside = (wanted >= 0) & (wanted < vocab_dev)
    picked = jnp.take(token_table, jnp.clip(wanted, 0, vocab_dev - 1), axis=0)
    own_rows = lax.psum_scatter(
        jnp.where(inside[:, None], picked.astype(jnp.float32), jnp.float32(0.0)),
        ("ctx", "head"),
        scatter_dimension=0,
        tiled=True,
    )
    prompt_rows = lax.all_gather(own_rows.astype(jnp.bfloat16), "head", axis=0, tiled=True)
    shift_scale = lax.dynamic_index_in_dim(modulation, step_index[0], 0, keepdims=False)
    modded = modulate(prompt_rows, shift_scale)
    text_mod = modded[:text_dev]
    concept_mod = modded[text_dev:]
    text_kv = jnp.einsum(
        "rd,dgc->rgc", text_mod, txt_qkv[:, 1:], preferred_element_type=jnp.float32
    )
    concept_qkv = jnp.einsum(
        "rd,dgc->rgc", concept_mod, txt_qkv, preferred_element_type=jnp.float32
    )
    text_keys = head_norm(text_kv[:, 0], qk_gain[1], head_dim).astype(jnp.bfloat16)
    text_values = text_kv[:, 1].astype(jnp.bfloat16)
    concept_queries = head_norm(concept_qkv[:, 0], qk_gain[0], head_dim).astype(jnp.bfloat16)
    concept_keys = head_norm(concept_qkv[:, 1], qk_gain[1], head_dim).astype(jnp.bfloat16)
    concept_values = concept_qkv[:, 2].astype(jnp.bfloat16)
    local_kv = jnp.stack(
        [
            jnp.concatenate([text_keys, concept_keys], axis=0),
            jnp.concatenate([text_values, concept_values], axis=0),
        ]
    )
    prompt_kv = lax.all_gather(local_kv, "ctx", axis=1, tiled=True).reshape(
        2, n_ctx, text_dev + concept_dev, group, head_dim
    )
    text_part = prompt_kv[:, :, :text_dev].reshape(2, -1, group, head_dim)
    concept_part = prompt_kv[:, :, text_dev:].reshape(2, -1, group, head_dim)
    image_queries = img_q.reshape(-1, group, head_dim)
    concept_q3 = concept_queries.reshape(-1, group, head_dim)
    first = block_stats(image_queries, text_part[0], text_part[1])
    second = block_stats(concept_q3, concept_part[0], concept_part[1])
    start_stats = (
        jnp.concatenate([first[0], second[0]], axis=1),
        jnp.concatenate([first[1], second[1]], axis=1),
        jnp.concatenate([first[2], second[2]], axis=1),
    )
    all_queries = jnp.concatenate([image_queries, concept_q3], axis=0)
    keys = lax.all_gather(img_k, "ctx", axis=0, tiled=True).reshape(-1, group, head_dim)
    values = lax.all_gather(img_v, "ctx", axis=0, tiled=True).reshape(-1, group, head_dim)
    peak, total, summed = combine_stats(start_stats, block_stats(all_queries, keys, values))
    attended = (
        jnp.transpose(summed / total[:, :, None], (1, 0, 2))
        .reshape(all_queries.shape[0], -1)
        .astype(jnp.bfloat16)
    )
    img_rows = img_q.shape[0]
    img_out = attended[:img_rows]
    concept_out = attended[img_rows:]
    concept_all = lax.all_gather(concept_out, "ctx", axis=0, tiled=True)
    dots = lax.dot_general(
        concept_all, img_out, (((1,), (1,)), ((), ())), preferred_element_type=jnp.float32
    )
    image_f = img_out.astype(jnp.float32)
    concept_f = concept_all.astype(jnp.float32)
    image_sq = jnp.sum(image_f * image_f, axis=1)
    concept_sq = jnp.sum(concept_f * concept_f, axis=1)
    width = group * head_dim * n_head
    dots_total, image_total, concept_total = (
        lax.psum(dots.astype(jnp.bfloat16), "head").astype(jnp.float32),
        lax.psum(image_sq.astype(jnp.bfloat16), "head").astype(jnp.float32),
        lax.psum(concept_sq.astype(jnp.bfloat16), "head").astype(jnp.float32),
    )
    saliency = scaled_scores(dots_total, concept_total, image_total, width)
    return (img_out, saliency)


def solution(mesh):
    return jax.shard_map(
        on_device,
        mesh=mesh,
        in_specs=(
            P("ctx", "head"),
            P("ctx", "head"),
            P("ctx", "head"),
            P(),
            P(),
            P(),
            P(("ctx", "head"), None),
            P(),
            P(None, None, "head"),
            P(),
        ),
        out_specs=(P("ctx", "head"), P(None, "ctx")),
        check_vma=False,
    )
```

profile of v0, /device:TPU:1, one launch (start us, length us, event | category | flops | bytes accessed | tf_op | source)
XLA Modules:
  0.0 1056.3 jit_solution(17856083692698793807)
XLA Ops:
  10.2 8.3 gather_fusion
  18.5 15.4 %convert_select_fusion = f32[1536,3072]{1,0:T(8,128)} fusion(bf16[1536,3072]{1,0:T(8,128)(2,1)} %gather_fusion, pred[1536]{0:T(1024)(128)(4,1)S(1)} %compare_and_fusion.1, pred[1536]{0:T(1024)(128)(4,1)S(1)} %and.20), kind=kLoop, calls=%fused_computation.1 | loop fusion | flops 14155776 | bytes 28314624 | tf_op jit(solution)/shard_map/jit(_where)/select_n | solution.py:68
  34.0 558.0 %fusion = f32[16,3072]{1,0:T(8,128)S(1)} fusion(f32[1536,3072]{1,0:T(8,128)} %convert_select_fusion), kind=kCustom, calls=%all-reduce-scatter | all-reduce-scatter fusion | flops 6291457 | bytes 19070976
  592.0 3.3 collective-permute-start
  596.7 6.8 collective-permute-start.1
  606.4 5.0 collective-permute-start.12
  617.7 3.1 collective-permute-start.17
  624.7 4.9 collective-permute-start.2
  629.6 2.8 collective-permute-start.20
  633.8 4.1 collective-permute-start.22
  639.9 2.6 collective-permute-start.24
  642.5 2.5 collective-permute-start.25
  645.0 2.6 collective-permute-start.26
  655.2 3.8 collective-permute-start.30
  660.8 5.3 collective-permute-start.5
  666.2 3.1 collective-permute-start.6
  669.2 3.1 collective-permute-start.7
  672.4 5.8 collective-permute-start.8
  682.7 75.6 %concatenate.47 = bf16[524,3072]{1,0:T(8,128)(2,1)} concatenate(bf16[12,3072]{1,0:T(8,128)(2,1)S(1)} %collective-permute-done.31, bf16[16,3072]{1,0:T(8,128)(2,1)S(1)} %collective-permute-done.30, bf16[16,3072]{1,0:T(8,128)(2,1)S(1)} %collective-permute-done.29, bf16[16,3072]{1,0:T(8,128)(2,1)S(1)} %collective-permute-done.28, bf16[16,3072]{1,0:T(8,128)(2,1)S(1)} %collective-permute-done.27, ...), dimensions={0} | concatenate | bytes 6537216
  759.3 6.0 all-gather
  765.9 7.0 fusion.39
  773.0 5.0 fusion.1
  779.6 4.7 copy.45
  784.3 4.8 copy.47
  789.1 2.6 fusion.62
  793.5 92.2 %all-gather.6.cloned.1.call-done = bf16[2,1536,768]{2,1,0:T(8,128)(2,1)} async-done(((bf16[2,24,768]{2,1,0:T(8,128)(2,1)}), bf16[2,1536,768]{2,1,0:T(8,128)(2,1)}) %all-gather.6.cloned.1.call-update) | async-done | bytes 4718608 | tf_op jit(solution)/shard_map/all_gather | solution.py:95
  885.7 10.8 %reshape.244 = bf16[2,64,24,6,128]{4,3,2,1,0:T(8,128)(2,1)} reshape(bf16[2,1536,768]{2,1,0:T(8,128)(2,1)} %all-gather.6.cloned.1.call-done) | data formatting | bytes 9437184 | tf_op jit(solution)/shard_map/reshape | solution.py:95
  898.5 3.1 fusion.60
  908.0 102.0 %all-gather.12.cloned.1.call-done = bf16[1024,768]{1,0:T(8,128)(2,1)} async-done(((bf16[16,768]{1,0:T(8,128)(2,1)}), bf16[1024,768]{1,0:T(8,128)(2,1)}) %all-gather.12.cloned.1.call-update) | async-done | bytes 1572880 | tf_op jit(solution)/shard_map/all_gather | solution.py:121
  1011.8 5.3 all-reduce.2
  1017.1 2.6 convolution_convert_fusion
  1019.7 28.5 %all-reduce.5.cloned.1.call-done = bf16[1024,32]{0,1:T(8,128)(2,1)} async-done(((bf16[1024,32]{0,1:T(8,128)(2,1)}), bf16[1024,32]{0,1:T(8,128)(2,1)}) %all-reduce.5.cloned.1.call-update) | async-done | bytes 65552 | tf_op jit(solution)/shard_map/psum | solution.py:131
  (141 shorter events, 50.6 us)
Async XLA Ops:
  7.2 772.5 %all-gather.8.cloned.1.call-start = ((), (), s32[]{:S(2)}) async-start(), calls=%async_computation.1 | async-start | bytes 3194880 | tf_op jit(solution)/shard_map/all_gather | solution.py:110
  7.9 776.4 %all-gather.10.cloned.1.call-start = ((), (), s32[]{:S(2)}) async-start(), calls=%async_computation.2 | async-start | bytes 3194880 | tf_op jit(solution)/shard_map/all_gather | solution.py:111
  592.0 19.3 %collective-permute-start = (bf16[16,3072]{1,0:T(8,128)(2,1)S(1)}, bf16[16,3072]{1,0:T(8,128)(2,1)S(1)}, u32[]{:S(2)}, u32[]{:S(2)}) collective-permute-start(bf16[16,3072]{1,0:T(8,128)(2,1)S(1)} %convert.77), channel_id=1, source_target_pairs={{0,1},{1,2},{2,3},{3,4},{4,5},{5,6},{6,7},{7,8},{8,9},{9,10},{10,1... | collective-permute-start | bytes 294920
  595.3 11.0 %collective-permute-start.31 = (bf16[12,3072]{1,0:T(8,128)(2,1)S(1)}, bf16[12,3072]{1,0:T(8,128)(2,1)S(1)}, u32[]{:S(2)}, u32[]{:S(2)}) collective-permute-start(bf16[12,3072]{1,0:T(8,128)(2,1)S(1)} %slice.110), channel_id=1, source_target_pairs={{0,32},{1,33},{2,34},{3,35},{4,36},{5,37},{6,38},{7,39},{8,40},{9,... | collective-permute-start | bytes 221192
  596.7 289.0 %all-gather.6.cloned.1.call-start = ((), (), s32[]{:S(2)}) async-start(), calls=%async_computation | async-start | bytes 4792320 | tf_op jit(solution)/shard_map/all_gather | solution.py:95
  596.7 16.0 %collective-permute-start.1 = (bf16[16,3072]{1,0:T(8,128)(2,1)S(1)}, bf16[16,3072]{1,0:T(8,128)(2,1)S(1)}, u32[]{:S(2)}, u32[]{:S(2)}) collective-permute-start(bf16[16,3072]{1,0:T(8,128)(2,1)S(1)} %convert.77), channel_id=1, source_target_pairs={{0,2},{1,3},{2,4},{3,5},{4,6},{5,7},{6,8},{7,9},{8,10},{9,11},{10,... | collective-permute-start | bytes 294920
  603.5 10.5 collective-permute-start.10
  604.8 11.1 %collective-permute-start.11 = (bf16[16,3072]{1,0:T(8,128)(2,1)S(1)}, bf16[16,3072]{1,0:T(8,128)(2,1)S(1)}, u32[]{:S(2)}, u32[]{:S(2)}) collective-permute-start(bf16[16,3072]{1,0:T(8,128)(2,1)S(1)} %convert.77), channel_id=1, source_target_pairs={{0,12},{1,13},{2,14},{3,15},{4,16},{5,17},{6,18},{7,19},{8,20},{9,... | collective-permute-start | bytes 294920
  606.4 11.3 %collective-permute-start.12 = (bf16[16,3072]{1,0:T(8,128)(2,1)S(1)}, bf16[16,3072]{1,0:T(8,128)(2,1)S(1)}, u32[]{:S(2)}, u32[]{:S(2)}) collective-permute-start(bf16[16,3072]{1,0:T(8,128)(2,1)S(1)} %convert.77), channel_id=1, source_target_pairs={{0,13},{1,14},{2,15},{3,16},{4,17},{5,18},{6,19},{7,20},{8,21},{9,... | collective-permute-start | bytes 294920
  614.0 10.7 %collective-permute-start.15 = (bf16[16,3072]{1,0:T(8,128)(2,1)S(1)}, bf16[16,3072]{1,0:T(8,128)(2,1)S(1)}, u32[]{:S(2)}, u32[]{:S(2)}) collective-permute-start(bf16[16,3072]{1,0:T(8,128)(2,1)S(1)} %convert.77), channel_id=1, source_target_pairs={{0,16},{1,17},{2,18},{3,19},{4,20},{5,21},{6,22},{7,23},{8,24},{9,... | collective-permute-start | bytes 294920
  616.0 13.6 %collective-permute-start.16 = (bf16[16,3072]{1,0:T(8,128)(2,1)S(1)}, bf16[16,3072]{1,0:T(8,128)(2,1)S(1)}, u32[]{:S(2)}, u32[]{:S(2)}) collective-permute-start(bf16[16,3072]{1,0:T(8,128)(2,1)S(1)} %convert.77), channel_id=1, source_target_pairs={{0,17},{1,18},{2,19},{3,20},{4,21},{5,22},{6,23},{7,24},{8,25},{9,... | collective-permute-start | bytes 294920
  617.7 14.7 %collective-permute-start.17 = (bf16[16,3072]{1,0:T(8,128)(2,1)S(1)}, bf16[16,3072]{1,0:T(8,128)(2,1)S(1)}, u32[]{:S(2)}, u32[]{:S(2)}) collective-permute-start(bf16[16,3072]{1,0:T(8,128)(2,1)S(1)} %convert.77), channel_id=1, source_target_pairs={{0,18},{1,19},{2,20},{3,21},{4,22},{5,23},{6,24},{7,25},{8,26},{9,... | collective-permute-start | bytes 294920
  620.8 13.0 %collective-permute-start.18 = (bf16[16,3072]{1,0:T(8,128)(2,1)S(1)}, bf16[16,3072]{1,0:T(8,128)(2,1)S(1)}, u32[]{:S(2)}, u32[]{:S(2)}) collective-permute-start(bf16[16,3072]{1,0:T(8,128)(2,1)S(1)} %convert.77), channel_id=1, source_target_pairs={{0,19},{1,20},{2,21},{3,22},{4,23},{5,24},{6,25},{7,26},{8,27},{9,... | collective-permute-start | bytes 294920
  623.0 15.5 %collective-permute-start.19 = (bf16[16,3072]{1,0:T(8,128)(2,1)S(1)}, bf16[16,3072]{1,0:T(8,128)(2,1)S(1)}, u32[]{:S(2)}, u32[]{:S(2)}) collective-permute-start(bf16[16,3072]{1,0:T(8,128)(2,1)S(1)} %convert.77), channel_id=1, source_target_pairs={{0,20},{1,21},{2,22},{3,23},{4,24},{5,25},{6,26},{7,27},{8,28},{9,... | collective-permute-start | bytes 294920
  624.7 15.2 %collective-permute-start.2 = (bf16[16,3072]{1,0:T(8,128)(2,1)S(1)}, bf16[16,3072]{1,0:T(8,128)(2,1)S(1)}, u32[]{:S(2)}, u32[]{:S(2)}) collective-permute-start(bf16[16,3072]{1,0:T(8,128)(2,1)S(1)} %convert.77), channel_id=1, source_target_pairs={{0,3},{1,4},{2,5},{3,6},{4,7},{5,8},{6,9},{7,10},{8,11},{9,12},{10... | collective-permute-start | bytes 294920
  629.6 12.9 %collective-permute-start.20 = (bf16[16,3072]{1,0:T(8,128)(2,1)S(1)}, bf16[16,3072]{1,0:T(8,128)(2,1)S(1)}, u32[]{:S(2)}, u32[]{:S(2)}) collective-permute-start(bf16[16,3072]{1,0:T(8,128)(2,1)S(1)} %convert.77), channel_id=1, source_target_pairs={{0,21},{1,22},{2,23},{3,24},{4,25},{5,26},{6,27},{7,28},{8,29},{9,... | collective-permute-start | bytes 294920
  632.4 12.6 %collective-permute-start.21 = (bf16[16,3072]{1,0:T(8,128)(2,1)S(1)}, bf16[16,3072]{1,0:T(8,128)(2,1)S(1)}, u32[]{:S(2)}, u32[]{:S(2)}) collective-permute-start(bf16[16,3072]{1,0:T(8,128)(2,1)S(1)} %convert.77), channel_id=1, source_target_pairs={{0,22},{1,23},{2,24},{3,25},{4,26},{5,27},{6,28},{7,29},{8,30},{9,... | collective-permute-start | bytes 294920
  633.8 13.8 %collective-permute-start.22 = (bf16[16,3072]{1,0:T(8,128)(2,1)S(1)}, bf16[16,3072]{1,0:T(8,128)(2,1)S(1)}, u32[]{:S(2)}, u32[]{:S(2)}) collective-permute-start(bf16[16,3072]{1,0:T(8,128)(2,1)S(1)} %convert.77), channel_id=1, source_target_pairs={{0,23},{1,24},{2,25},{3,26},{4,27},{5,28},{6,29},{7,30},{8,31},{9,... | collective-permute-start | bytes 294920
  638.5 11.2 %collective-permute-start.23 = (bf16[16,3072]{1,0:T(8,128)(2,1)S(1)}, bf16[16,3072]{1,0:T(8,128)(2,1)S(1)}, u32[]{:S(2)}, u32[]{:S(2)}) collective-permute-start(bf16[16,3072]{1,0:T(8,128)(2,1)S(1)} %convert.77), channel_id=1, source_target_pairs={{0,24},{1,25},{2,26},{3,27},{4,28},{5,29},{6,30},{7,31},{8,32},{9,... | collective-permute-start | bytes 294920
  639.9 11.8 %collective-permute-start.24 = (bf16[16,3072]{1,0:T(8,128)(2,1)S(1)}, bf16[16,3072]{1,0:T(8,128)(2,1)S(1)}, u32[]{:S(2)}, u32[]{:S(2)}) collective-permute-start(bf16[16,3072]{1,0:T(8,128)(2,1)S(1)} %convert.77), channel_id=1, source_target_pairs={{0,25},{1,26},{2,27},{3,28},{4,29},{5,30},{6,31},{7,32},{8,33},{9,... | collective-permute-start | bytes 294920
  642.5 10.4 collective-permute-start.25
  647.6 11.3 %collective-permute-start.27 = (bf16[16,3072]{1,0:T(8,128)(2,1)S(1)}, bf16[16,3072]{1,0:T(8,128)(2,1)S(1)}, u32[]{:S(2)}, u32[]{:S(2)}) collective-permute-start(bf16[16,3072]{1,0:T(8,128)(2,1)S(1)} %convert.77), channel_id=1, source_target_pairs={{0,28},{1,29},{2,30},{3,31},{4,32},{5,33},{6,34},{7,35},{8,36},{9,... | collective-permute-start | bytes 294920
  649.8 11.0 %collective-permute-start.28 = (bf16[16,3072]{1,0:T(8,128)(2,1)S(1)}, bf16[16,3072]{1,0:T(8,128)(2,1)S(1)}, u32[]{:S(2)}, u32[]{:S(2)}) collective-permute-start(bf16[16,3072]{1,0:T(8,128)(2,1)S(1)} %convert.77), channel_id=1, source_target_pairs={{0,29},{1,30},{2,31},{3,32},{4,33},{5,34},{6,35},{7,36},{8,37},{9,... | collective-permute-start | bytes 294920
  651.6 14.5 %collective-permute-start.29 = (bf16[16,3072]{1,0:T(8,128)(2,1)S(1)}, bf16[16,3072]{1,0:T(8,128)(2,1)S(1)}, u32[]{:S(2)}, u32[]{:S(2)}) collective-permute-start(bf16[16,3072]{1,0:T(8,128)(2,1)S(1)} %convert.77), channel_id=1, source_target_pairs={{0,30},{1,31},{2,32},{3,33},{4,34},{5,35},{6,36},{7,37},{8,38},{9,... | collective-permute-start | bytes 294920
  652.9 16.3 %collective-permute-start.3 = (bf16[16,3072]{1,0:T(8,128)(2,1)S(1)}, bf16[16,3072]{1,0:T(8,128)(2,1)S(1)}, u32[]{:S(2)}, u32[]{:S(2)}) collective-permute-start(bf16[16,3072]{1,0:T(8,128)(2,1)S(1)} %convert.77), channel_id=1, source_target_pairs={{0,4},{1,5},{2,6},{3,7},{4,8},{5,9},{6,10},{7,11},{8,12},{9,13},{1... | collective-permute-start | bytes 294920
  655.2 17.2 %collective-permute-start.30 = (bf16[16,3072]{1,0:T(8,128)(2,1)S(1)}, bf16[16,3072]{1,0:T(8,128)(2,1)S(1)}, u32[]{:S(2)}, u32[]{:S(2)}) collective-permute-start(bf16[16,3072]{1,0:T(8,128)(2,1)S(1)} %convert.77), channel_id=1, source_target_pairs={{0,31},{1,32},{2,33},{3,34},{4,35},{5,36},{6,37},{7,38},{8,39},{9,... | collective-permute-start | bytes 294920
  659.0 19.2 %collective-permute-start.4 = (bf16[16,3072]{1,0:T(8,128)(2,1)S(1)}, bf16[16,3072]{1,0:T(8,128)(2,1)S(1)}, u32[]{:S(2)}, u32[]{:S(2)}) collective-permute-start(bf16[16,3072]{1,0:T(8,128)(2,1)S(1)} %convert.77), channel_id=1, source_target_pairs={{0,5},{1,6},{2,7},{3,8},{4,9},{5,10},{6,11},{7,12},{8,13},{9,14},{... | collective-permute-start | bytes 294920
  660.8 19.3 %collective-permute-start.5 = (bf16[16,3072]{1,0:T(8,128)(2,1)S(1)}, bf16[16,3072]{1,0:T(8,128)(2,1)S(1)}, u32[]{:S(2)}, u32[]{:S(2)}) collective-permute-start(bf16[16,3072]{1,0:T(8,128)(2,1)S(1)} %convert.77), channel_id=1, source_target_pairs={{0,6},{1,7},{2,8},{3,9},{4,10},{5,11},{6,12},{7,13},{8,14},{9,15},... | collective-permute-start | bytes 294920
  666.2 14.0 %collective-permute-start.6 = (bf16[16,3072]{1,0:T(8,128)(2,1)S(1)}, bf16[16,3072]{1,0:T(8,128)(2,1)S(1)}, u32[]{:S(2)}, u32[]{:S(2)}) collective-permute-start(bf16[16,3072]{1,0:T(8,128)(2,1)S(1)} %convert.77), channel_id=1, source_target_pairs={{0,7},{1,8},{2,9},{3,10},{4,11},{5,12},{6,13},{7,14},{8,15},{9,16}... | collective-permute-start | bytes 294920
  669.2 10.9 %collective-permute-start.7 = (bf16[16,3072]{1,0:T(8,128)(2,1)S(1)}, bf16[16,3072]{1,0:T(8,128)(2,1)S(1)}, u32[]{:S(2)}, u32[]{:S(2)}) collective-permute-start(bf16[16,3072]{1,0:T(8,128)(2,1)S(1)} %convert.77), channel_id=1, source_target_pairs={{0,8},{1,9},{2,10},{3,11},{4,12},{5,13},{6,14},{7,15},{8,16},{9,17... | collective-permute-start | bytes 294920
  779.0 230.9 %all-gather.12.cloned.1.call-start = ((), (), s32[]{:S(2)}) async-start(), calls=%async_computation.3 | async-start | bytes 1597440 | tf_op jit(solution)/shard_map/all_gather | solution.py:121
  907.8 140.4 %all-reduce.5.cloned.1.call-start = ((), (), s32[]{:S(2)}) async-start(), calls=%async_computation.4 | async-start | bytes 131072 | tf_op jit(solution)/shard_map/psum | solution.py:131
  (13 other events, 970.1 us)
Sparse Core Ops, SparseCore 0:
  9.7 112.7 all-gather.7
  596.8 116.6 all-gather.9
  779.1 106.5 all-gather.5
  907.9 101.9 all-gather.11
  1019.8 28.3 all-reduce.4
where the time goes:
time: 1060 us
  blocking collectives  569 us (54%)
  waiting for transfers between devices  226 us (21%)
  local copies, waits for them, and re-layouts  117 us (11%)
  starting transfers between devices  86.4 us (8%)
  other arithmetic  22.4 us (2%)
  matrix products  20.1 us (2%)
  between operations  15.3 us (1%)
    unnamed x1, blocking collectives  558 us
    all_gather x1, waiting for transfers between devices, on_device(): concept_all = lax.all_gather(concept_out, 'ctx', axis=0, tiled=True)  102 us
    all_gather x1, waiting for transfers between devices, on_device(): lax.all_gather(local_kv, 'ctx', axis=1, tiled=True)  92.2 us
    unnamed x32, starting transfers between devices  85.9 us
    unnamed x19, local copies, waits for them, and re-layouts  79.7 us
    psum x1, waiting for transfers between devices, on_device(): lax.psum(dots.astype(jnp.bfloat16), 'head').astype(jnp.float32)  28.5 us
  transfers between devices with their start and end apart: 37, of which 5 were waited for; matrix products, arithmetic and copies ran while one was open for 65% of the time, Pallas kernels for 0%

commit v1 on v0

--- a/solution.py
+++ b/solution.py
@@ -47,6 +47,12 @@
     return dots / (jnp.sqrt(jnp.float32(width)) * concept_rms[:, None] * image_rms[None, :])
 
 
+def gather_ctx(block):
+    n_ctx = lax.axis_size("ctx")
+    spread = jnp.broadcast_to(block[None], (n_ctx,) + block.shape)
+    return lax.all_to_all(spread, "ctx", 0, 0, tiled=True)
+
+
 def on_device(
     img_q, img_k, img_v, txt_ids, concept_ids, step_index, token_table, modulation, txt_qkv, qk_gain
 ):
@@ -64,12 +70,12 @@
     wanted = combined - offset
     inside = (wanted >= 0) & (wanted < vocab_dev)
     picked = jnp.take(token_table, jnp.clip(wanted, 0, vocab_dev - 1), axis=0)
-    own_rows = lax.psum_scatter(
-        jnp.where(inside[:, None], picked.astype(jnp.float32), jnp.float32(0.0)),
-        ("ctx", "head"),
-        scatter_dimension=0,
-        tiled=True,
+    n_all = n_ctx * n_head
+    mine = jnp.where(inside[:, None], picked, jnp.zeros((), picked.dtype))
+    parts = lax.all_to_all(
+        mine.reshape(n_all, -1, mine.shape[1]), ("ctx", "head"), 0, 0, tiled=True
     )
+    own_rows = jnp.sum(parts.astype(jnp.float32), axis=0)
     prompt_rows = lax.all_gather(own_rows.astype(jnp.bfloat16), "head", axis=0, tiled=True)
     shift_scale = lax.dynamic_index_in_dim(modulation, step_index[0], 0, keepdims=False)
     modded = modulate(prompt_rows, shift_scale)
@@ -92,11 +98,9 @@
             jnp.concatenate([text_values, concept_values], axis=0),
         ]
     )
-    prompt_kv = lax.all_gather(local_kv, "ctx", axis=1, tiled=True).reshape(
-        2, n_ctx, text_dev + concept_dev, group, head_dim
-    )
-    text_part = prompt_kv[:, :, :text_dev].reshape(2, -1, group, head_dim)
-    concept_part = prompt_kv[:, :, text_dev:].reshape(2, -1, group, head_dim)
+    prompt_kv = gather_ctx(local_kv)
+    text_part = jnp.swapaxes(prompt_kv[:, :, :text_dev], 0, 1).reshape(2, -1, group, head_dim)
+    concept_part = jnp.swapaxes(prompt_kv[:, :, text_dev:], 0, 1).reshape(2, -1, group, head_dim)
     image_queries = img_q.reshape(-1, group, head_dim)
     concept_q3 = concept_queries.reshape(-1, group, head_dim)
     first = block_stats(image_queries, text_part[0], text_part[1])
@@ -118,7 +122,7 @@
     img_rows = img_q.shape[0]
     img_out = attended[:img_rows]
     concept_out = attended[img_rows:]
-    concept_all = lax.all_gather(concept_out, "ctx", axis=0, tiled=True)
+    concept_all = gather_ctx(concept_out).reshape(-1, concept_out.shape[1])
     dots = lax.dot_general(
         concept_all, img_out, (((1,), (1,)), ((), ())), preferred_element_type=jnp.float32
     )
@@ -127,11 +131,18 @@
     image_sq = jnp.sum(image_f * image_f, axis=1)
     concept_sq = jnp.sum(concept_f * concept_f, axis=1)
     width = group * head_dim * n_head
-    dots_total, image_total, concept_total = (
-        lax.psum(dots.astype(jnp.bfloat16), "head").astype(jnp.float32),
-        lax.psum(image_sq.astype(jnp.bfloat16), "head").astype(jnp.float32),
-        lax.psum(concept_sq.astype(jnp.bfloat16), "head").astype(jnp.float32),
-    )
+    sums = jnp.concatenate(
+        [
+            jnp.concatenate([dots, concept_sq[:, None]], axis=1),
+            jnp.concatenate([image_sq, jnp.zeros((1,), jnp.float32)])[None],
+        ]
+    ).astype(jnp.bfloat16)
+    other = lax.ppermute(sums, "head", [(0, 1), (1, 0)])
+    sums = sums.astype(jnp.float32) + other.astype(jnp.float32)
+    concepts = dots.shape[0]
+    dots_total = sums[:concepts, : img_rows]
+    concept_total = sums[:concepts, img_rows]
+    image_total = sums[concepts, :img_rows]
     saliency = scaled_scores(dots_total, concept_total, image_total, width)
     return (img_out, saliency)
 

time: 1060 us -> 490 us (0.46)
  blocking collectives: 569 us -> 10 us
  waiting for transfers between devices: 226 us -> 336 us
  local copies, waits for them, and re-layouts: 117 us -> 52.6 us
  starting transfers between devices: 86.4 us -> 27.6 us
    unnamed x1 -> x0, blocking collectives: 558 us -> none
    all_gather x2 -> x0, waiting for transfers between devices: 194 us -> none  [the longest x1 102 us: on_device(): concept_all = lax.all_gather(concept_out, 'ctx', axis=0, tiled=True)]
    all_to_all x0 -> x3, waiting for transfers between devices: none -> 192 us  [the longest x1 169 us: on_device(): lax.all_to_all(mine.reshape(n_all, -1, mine.shape[1]), ('ctx', 'head'), 0...]
    all_gather x1, waiting for transfers between devices: 0.01 us -> 132 us  [on_device(): lax.all_gather(img_v, 'ctx', axis=0, tiled=True)]
    unnamed x32 -> x0, starting transfers between devices: 85.9 us -> none
    unnamed x19 -> x14, local copies, waits for them, and re-layouts: 79.7 us -> 1.47 us
    psum x1 -> x0, waiting for transfers between devices: 28.5 us -> none  [on_device(): lax.psum(dots.astype(jnp.bfloat16), 'head').astype(jnp.float32)]
    all_to_all x0 -> x3, starting transfers between devices: none -> 25.8 us  [the longest x2 13.9 us: gather_ctx(): return lax.all_to_all(spread, 'ctx', 0, 0, tiled=True)]
  transfers between devices with their start and end apart: 37 -> 6, of which waited for: 5 -> 5; matrix products, arithmetic and copies ran while one was open for 65% -> 7% of each run, Pallas kernels for 0% -> 0%
where the time goes in v1:
time: 490 us; the launch traced here: 488 us
  waiting for transfers between devices  336 us (69%)
  local copies, waits for them, and re-layouts  52.6 us (11%)
  starting transfers between devices  27.6 us (6%)
  matrix products  24 us (5%)
  other arithmetic  22.6 us (5%)
  between operations  15 us (3%)
  blocking collectives  10 us (2%)
    all_to_all x1, waiting for transfers between devices, on_device(): lax.all_to_all(mine.reshape(n_all, -1, mine.shape[1]), ('ctx', 'head'), 0...  169 us
    all_gather x1, waiting for transfers between devices, on_device(): lax.all_gather(img_v, 'ctx', axis=0, tiled=True)  132 us
    all_to_all x2, waiting for transfers between devices, gather_ctx(): return lax.all_to_all(spread, 'ctx', 0, 0, tiled=True)  23.2 us
    gather x2, local copies, waits for them, and re-layouts, on_device(): picked = jnp.take(token_table, jnp.clip(wanted, 0, vocab_dev - 1), axis=0)  21.9 us
    all_to_all x2, starting transfers between devices, gather_ctx(): return lax.all_to_all(spread, 'ctx', 0, 0, tiled=True)  13.9 us
    all_to_all x1, starting transfers between devices, on_device(): lax.all_to_all(mine.reshape(n_all, -1, mine.shape[1]), ('ctx', 'head'), 0...  11.9 us
    select_n x1, other arithmetic, on_device(): mine = jnp.where(inside[:, None], picked, jnp.zeros((), picked.dtype))  11.2 us
    all_gather x1, blocking collectives, on_device(): lax.all_gather(own_rows.astype(jnp.bfloat16), 'head', axis=0, tiled=True)  10 us
  transfers between devices with their start and end apart: 6, of which 5 were waited for; matrix products, arithmetic and copies ran while one was open for 7% of the time, Pallas kernels for 0%

profile of v1, /device:TPU:1, one launch (start us, length us, event | category | flops | bytes accessed | tf_op | source)
XLA Modules:
  0.0 488.2 jit_solution(6876830155378695263)
XLA Ops:
  9.3 8.4 %gather_fusion = bf16[1536,3072]{1,0:T(8,128)(2,1)} fusion(bf16[256,3072]{1,0:T(8,128)(2,1)S(1)} %copy-done, s32[2048]{0:T(1024)S(1)} %pad_clamp_fusion), kind=kCustom, calls=%fused_computation | custom fusion | bytes 18880512 | tf_op jit(solution)/shard_map/jit(_take)/gather | solution.py:72
  17.7 13.5 %gather.7 = bf16[128,12,3072]{2,1,0:T(8,128)(2,1)} reshape(bf16[1536,3072]{1,0:T(8,128)(2,1)} %gather_fusion) | data formatting | bytes 18874368 | tf_op jit(solution)/shard_map/jit(_take)/gather | solution.py:72
  31.4 11.2 %select_select_fusion = bf16[128,12,3072]{2,1,0:T(8,128)(2,1)} fusion(bf16[128,12,3072]{2,1,0:T(8,128)(2,1)} %gather.7, pred[128,12]{1,0:T(8,128)(4,1)S(1)} %compare_and_fusion, pred[128,12]{1,0:T(8,128)(4,1)S(1)} %and.21), kind=kLoop, calls=%fused_computation.1 | loop fusion | flops 9437184 | bytes 18877440 | tf_op jit(solution)/shard_map/jit(_where)/select_n | solution.py:74
  42.7 11.9 %all-to-all-start = ((bf16[128,12,3072]{2,1,0:T(8,128)(2,1)}), bf16[128,12,3072]{2,1,0:T(8,128)(2,1)}, u32[]{:S(2)}, u32[]{:S(2)}) async-start(bf16[128,12,3072]{2,1,0:T(8,128)(2,1)} %select_select_fusion), calls=%async_computation | async-start | bytes 25165824 | tf_op jit(solution)/shard_map/all_to_all | solution.py:75
  57.6 168.6 %all-to-all-done = bf16[128,12,3072]{2,1,0:T(8,128)(2,1)} async-done(((bf16[128,12,3072]{2,1,0:T(8,128)(2,1)}), bf16[128,12,3072]{2,1,0:T(8,128)(2,1)}, u32[]{:S(2)}, u32[]{:S(2)}) %all-to-all-start) | async-done | bytes 9437216 | tf_op jit(solution)/shard_map/all_to_all | solution.py:75
  226.2 7.0 %reduce_sum.102 = bf16[12,3072]{1,0:T(8,128)(2,1)S(1)} reduce(bf16[128,12,3072]{2,1,0:T(8,128)(2,1)} %all-to-all-done, bf16[]{:T(256)} %constant.27.clone.1), dimensions={0}, to_apply=%region_0.1 | reduce | flops 4681728 | bytes 9510914 | tf_op jit(solution)/shard_map/reduce_sum | solution.py:78
  233.2 10.0 %all-gather = bf16[2,12,3072]{2,1,0:T(8,128)(2,1)S(1)} all-gather(bf16[1,12,3072]{2,1,0:T(8,128)(2,1)S(1)} %bitcast.111), channel_id=1, replica_groups=mesh['ctx'=64,'head'=2] {'head'}, dimensions={0}, use_global_device_ids=true | all-gather | bytes 221184 | tf_op jit(solution)/shard_map/all_gather | solution.py:79
  243.8 7.0 %fusion.41 = f32[16,3,768]{2,0,1:T(8,128)S(1)} fusion(bf16[3072,3,768]{2,0,1:T(8,128)(2,1)} %param.18, bf16[24,3072]{1,0:T(8,128)(2,1)S(1)} %add_convert_fusion), kind=kOutput, calls=%fused_computation.44 | convolution fusion | flops 226492416 | bytes 14401536 | tf_op jit(solution)/shard_map/rd,dgc->rgc/dot_general | solution.py:87
  250.9 5.0 %fusion = f32[8,2,768]{2,0,1:T(8,128)S(1)} fusion(bf16[3072,3,768]{2,0,1:T(8,128)(2,1)} %param.18, bf16[24,3072]{1,0:T(8,128)(2,1)S(1)} %add_convert_fusion), kind=kOutput, calls=%fused_computation.2 | convolution fusion | flops 75497472 | bytes 9535488 | tf_op jit(solution)/shard_map/rd,dgc->rgc/dot_general | solution.py:84
  256.3 2.5 broadcast_in_dim.36
  258.7 8.2 %all-to-all-start.1 = ((bf16[64,2,24,768]{3,2,1,0:T(8,128)(2,1)}), bf16[64,2,24,768]{3,2,1,0:T(8,128)(2,1)}, u32[]{:S(2)}, u32[]{:S(2)}) async-start(bf16[64,2,24,768]{3,2,1,0:T(8,128)(2,1)} %broadcast_in_dim.36), calls=%async_computation.1 | async-start | bytes 9437184 | tf_op jit(solution)/shard_map/all_to_all | solution.py:53
  267.0 7.4 %all-gather.4.cloned.1.call-done = bf16[2048,768]{1,0:T(8,128)(2,1)} async-done(((bf16[32,768]{1,0:T(8,128)(2,1)}), bf16[2048,768]{1,0:T(8,128)(2,1)}) %all-gather.4.cloned.1.call-update) | async-done | bytes 3145744 | tf_op jit(solution)/shard_map/all_gather | solution.py:114
  274.4 4.7 copy.63
  279.1 131.9 %all-gather.6.cloned.1.call-done = bf16[2048,768]{1,0:T(8,128)(2,1)} async-done(((bf16[32,768]{1,0:T(8,128)(2,1)}), bf16[2048,768]{1,0:T(8,128)(2,1)}) %all-gather.6.cloned.1.call-update) | async-done | bytes 3145744 | tf_op jit(solution)/shard_map/all_gather | solution.py:115
  411.0 4.7 copy.65
  416.0 2.6 fusion.69
  418.5 1.4 copy-done.2
  420.4 1.5 slice_bitcast_fusion.1
  422.0 1.0 fusion.68
  423.0 0.9 squeeze.23
  424.3 2.1 slice_bitcast_fusion
  426.7 2.8 squeeze.25
  429.5 2.2 fusion.70
  431.7 2.0 squeeze.24
  434.2 2.8 squeeze.26
  437.3 2.1 fusion.4
  439.4 3.9 fusion.27
  443.3 1.3 broadcast_in_dim.37
  444.6 5.7 %all-to-all-start.2 = ((bf16[64,16,768]{2,1,0:T(8,128)(2,1)}), bf16[64,16,768]{2,1,0:T(8,128)(2,1)S(1)}, u32[]{:S(2)}, u32[]{:S(2)}) async-start(bf16[64,16,768]{2,1,0:T(8,128)(2,1)} %broadcast_in_dim.37), calls=%async_computation.2 | async-start | bytes 3145728 | tf_op jit(solution)/shard_map/all_to_all | solution.py:53
  450.6 23.2 %all-to-all-done.2 = bf16[64,16,768]{2,1,0:T(8,128)(2,1)S(1)} async-done(((bf16[64,16,768]{2,1,0:T(8,128)(2,1)}), bf16[64,16,768]{2,1,0:T(8,128)(2,1)S(1)}, u32[]{:S(2)}, u32[]{:S(2)}) %all-to-all-start.2) | async-done | bytes 1572896 | tf_op jit(solution)/shard_map/all_to_all | solution.py:53
  474.8 1.7 collective-permute-start
  476.5 3.9 collective-permute-done
  (80 shorter events, 10.2 us)
Async XLA Ops:
  7.2 2.2 copy-start
  42.7 14.0 %copy-start.6 = (f32[2,128]{1,0:T(2,128)S(1)}, f32[2,128]{1,0:T(2,128)}, u32[]{:S(2)}) copy-start(f32[2,128]{1,0:T(2,128)} %param.19) | copy-start | bytes 3076
  42.7 183.5 %all-to-all-start = ((bf16[128,12,3072]{2,1,0:T(8,128)(2,1)}), bf16[128,12,3072]{2,1,0:T(8,128)(2,1)}, u32[]{:S(2)}, u32[]{:S(2)}) async-start(bf16[128,12,3072]{2,1,0:T(8,128)(2,1)} %select_select_fusion), calls=%async_computation | async-start | bytes 25165824 | tf_op jit(solution)/shard_map/all_to_all | solution.py:75
  54.6 219.8 %all-gather.4.cloned.1.call-start = ((), (), s32[]{:S(2)}) async-start(), calls=%async_computation.3 | async-start | bytes 3194880 | tf_op jit(solution)/shard_map/all_gather | solution.py:114
  55.3 355.7 %all-gather.6.cloned.1.call-start = ((), (), s32[]{:S(2)}) async-start(), calls=%async_computation.4 | async-start | bytes 3194880 | tf_op jit(solution)/shard_map/all_gather | solution.py:115
  258.7 8.2 %copy-start.5 = (bf16[32,768]{1,0:T(8,128)(2,1)S(1)}, bf16[32,768]{1,0:T(8,128)(2,1)}, u32[]{:S(2)}) copy-start(bf16[32,768]{1,0:T(8,128)(2,1)} %param.10) | copy-start | bytes 147460
  258.7 161.7 %all-to-all-start.1 = ((bf16[64,2,24,768]{3,2,1,0:T(8,128)(2,1)}), bf16[64,2,24,768]{3,2,1,0:T(8,128)(2,1)}, u32[]{:S(2)}, u32[]{:S(2)}) async-start(bf16[64,2,24,768]{3,2,1,0:T(8,128)(2,1)} %broadcast_in_dim.36), calls=%async_computation.1 | async-start | bytes 9437184 | tf_op jit(solution)/shard_map/all_to_all | solution.py:53
  416.0 4.5 copy-start.3
  418.5 1.4 copy-start.2
  443.3 38.0 %copy-start.1 = (bf16[256,3072]{1,0:T(8,128)(2,1)S(1)}, bf16[256,3072]{1,0:T(8,128)(2,1)}, u32[]{:S(2)}) copy-start(bf16[256,3072]{1,0:T(8,128)(2,1)} %param.16) | copy-start | bytes 4718596
  444.6 29.2 %all-to-all-start.2 = ((bf16[64,16,768]{2,1,0:T(8,128)(2,1)}), bf16[64,16,768]{2,1,0:T(8,128)(2,1)S(1)}, u32[]{:S(2)}, u32[]{:S(2)}) async-start(bf16[64,16,768]{2,1,0:T(8,128)(2,1)} %broadcast_in_dim.37), calls=%async_computation.2 | async-start | bytes 3145728 | tf_op jit(solution)/shard_map/all_to_all | solution.py:53
  450.4 31.0 %copy-start.4 = (bf16[32,768]{1,0:T(8,128)(2,1)}, bf16[32,768]{1,0:T(8,128)(2,1)S(1)}, u32[]{:S(2)}) copy-start(bf16[32,768]{1,0:T(8,128)(2,1)S(1)} %get-tuple-element.3) | copy-start | bytes 147460
  474.8 5.6 %collective-permute-start = (bf16[1025,33]{0,1:T(8,128)(2,1)S(1)}, bf16[1025,33]{0,1:T(8,128)(2,1)S(1)}, u32[]{:S(2)}, u32[]{:S(2)}) collective-permute-start(bf16[1025,33]{0,1:T(8,128)(2,1)S(1)} %pad_maximum_fusion), channel_id=1, source_target_pairs={{0,1},{1,0},{2,3},{3,2},{4,5},{5,4},{6,7},{7,6},{8,9},{9,8},{10,11... | collective-permute-start | bytes 202958 | tf_op jit(solution)/shard_map/ppermute | solution.py:140
Sparse Core Ops, SparseCore 0:
  57.1 217.2 all-gather.3
  276.1 134.8 all-gather.5

commit v2 on v1

v2 whole, which is shorter than its diff:
```python
import math

import jax
import jax.numpy as jnp
from jax import lax
from jax.experimental import pallas as pl
from jax.experimental.pallas import tpu as pltpu
from jax.sharding import PartitionSpec as P

BF = jnp.bfloat16
F32 = jnp.float32
HD = 128
SLOTS = 32
CON = 112
TXT = 64
ROWS = CON + TXT
MIB = 1 << 20


def modulate(rows, shift_scale):
    values = rows.astype(F32)
    mean = jnp.mean(values, axis=1, keepdims=True)
    centered = values - mean
    var = jnp.mean(centered * centered, axis=1, keepdims=True)
    normed = centered * lax.rsqrt(var + 1e-06)
    return (normed * (1.0 + shift_scale[1]) + shift_scale[0]).astype(BF)


def head_norm(values, gain, head_dim):
    shaped = values.reshape(values.shape[0], -1, head_dim)
    meansq = jnp.mean(shaped * shaped, axis=2, keepdims=True)
    return (shaped * lax.rsqrt(meansq + 1e-06) * gain).reshape(values.shape[0], -1)


def block_stats(queries, keys, values):
    scores = jnp.einsum("rgd,kgd->grk", queries, keys, preferred_element_type=F32)
    scores = scores * queries.shape[-1] ** (-0.5)
    peak = jnp.max(scores, axis=2)
    weights = jnp.exp(scores - peak[:, :, None])
    total = jnp.sum(weights, axis=2)
    summed = jnp.einsum("grk,kgd->grd", weights.astype(BF), values, preferred_element_type=F32)
    return (peak, total, summed)


def combine_stats(first, second):
    peak = jnp.maximum(first[0], second[0])
    left = jnp.exp(first[0] - peak)
    right = jnp.exp(second[0] - peak)
    total = first[1] * left + second[1] * right
    summed = first[2] * left[:, :, None] + second[2] * right[:, :, None]
    return (peak, total, summed)


def scaled_scores(dots, concept_sq, image_sq, width):
    concept_rms = jnp.sqrt(concept_sq / width + 1e-06)
    image_rms = jnp.sqrt(image_sq / width + 1e-06)
    return dots / (jnp.sqrt(F32(width)) * concept_rms[:, None] * image_rms[None, :])


def gather_ctx(block):
    n_ctx = lax.axis_size("ctx")
    spread = jnp.broadcast_to(block[None], (n_ctx,) + block.shape)
    return lax.all_to_all(spread, "ctx", 0, 0, tiled=True)


def general(
    img_q, img_k, img_v, txt_ids, concept_ids, step_index, token_table, modulation, txt_qkv, qk_gain
):
    n_ctx = lax.axis_size("ctx")
    n_head = lax.axis_size("head")
    head_dim = qk_gain.shape[1]
    group = img_q.shape[1] // head_dim
    text_dev = txt_ids.shape[0] // n_ctx
    concept_dev = concept_ids.shape[0] // n_ctx
    vocab_dev = token_table.shape[0]
    combined = jnp.concatenate(
        [txt_ids.reshape(n_ctx, text_dev), concept_ids.reshape(n_ctx, concept_dev)], axis=1
    ).reshape(-1)
    offset = lax.axis_index(("ctx", "head")) * vocab_dev
    wanted = combined - offset
    inside = (wanted >= 0) & (wanted < vocab_dev)
    picked = jnp.take(token_table, jnp.clip(wanted, 0, vocab_dev - 1), axis=0)
    n_all = n_ctx * n_head
    mine = jnp.where(inside[:, None], picked, jnp.zeros((), picked.dtype))
    parts = lax.all_to_all(
        mine.reshape(n_all, -1, mine.shape[1]), ("ctx", "head"), 0, 0, tiled=True
    )
    own_rows = jnp.sum(parts.astype(F32), axis=0)
    prompt_rows = lax.all_gather(own_rows.astype(BF), "head", axis=0, tiled=True)
    shift_scale = lax.dynamic_index_in_dim(modulation, step_index[0], 0, keepdims=False)
    modded = modulate(prompt_rows, shift_scale)
    text_mod = modded[:text_dev]
    concept_mod = modded[text_dev:]
    text_kv = jnp.einsum("rd,dgc->rgc", text_mod, txt_qkv[:, 1:], preferred_element_type=F32)
    concept_qkv = jnp.einsum("rd,dgc->rgc", concept_mod, txt_qkv, preferred_element_type=F32)
    text_keys = head_norm(text_kv[:, 0], qk_gain[1], head_dim).astype(BF)
    text_values = text_kv[:, 1].astype(BF)
    concept_queries = head_norm(concept_qkv[:, 0], qk_gain[0], head_dim).astype(BF)
    concept_keys = head_norm(concept_qkv[:, 1], qk_gain[1], head_dim).astype(BF)
    concept_values = concept_qkv[:, 2].astype(BF)
    local_kv = jnp.stack(
        [
            jnp.concatenate([text_keys, concept_keys], axis=0),
            jnp.concatenate([text_values, concept_values], axis=0),
        ]
    )
    prompt_kv = gather_ctx(local_kv)
    text_part = jnp.swapaxes(prompt_kv[:, :, :text_dev], 0, 1).reshape(2, -1, group, head_dim)
    concept_part = jnp.swapaxes(prompt_kv[:, :, text_dev:], 0, 1).reshape(2, -1, group, head_dim)
    image_queries = img_q.reshape(-1, group, head_dim)
    concept_q3 = concept_queries.reshape(-1, group, head_dim)
    first = block_stats(image_queries, text_part[0], text_part[1])
    second = block_stats(concept_q3, concept_part[0], concept_part[1])
    start_stats = (
        jnp.concatenate([first[0], second[0]], axis=1),
        jnp.concatenate([first[1], second[1]], axis=1),
        jnp.concatenate([first[2], second[2]], axis=1),
    )
    all_queries = jnp.concatenate([image_queries, concept_q3], axis=0)
    image_kv = gather_ctx(jnp.stack([img_k, img_v]))
    keys = image_kv[:, 0].reshape(-1, group, head_dim)
    values = image_kv[:, 1].reshape(-1, group, head_dim)
    peak, total, summed = combine_stats(start_stats, block_stats(all_queries, keys, values))
    attended = (
        jnp.transpose(summed / total[:, :, None], (1, 0, 2))
        .reshape(all_queries.shape[0], -1)
        .astype(BF)
    )
    img_rows = img_q.shape[0]
    img_out = attended[:img_rows]
    concept_out = attended[img_rows:]
    concept_all = gather_ctx(concept_out).reshape(-1, concept_out.shape[1])
    dots = lax.dot_general(
        concept_all, img_out, (((1,), (1,)), ((), ())), preferred_element_type=F32
    )
    image_f = img_out.astype(F32)
    concept_f = concept_all.astype(F32)
    image_sq = jnp.sum(image_f * image_f, axis=1)
    concept_sq = jnp.sum(concept_f * concept_f, axis=1)
    width = group * head_dim * n_head
    sums = jnp.concatenate(
        [
            jnp.concatenate([dots, concept_sq[:, None]], axis=1),
            jnp.concatenate([image_sq, jnp.zeros((1,), F32)])[None],
        ]
    ).astype(BF)
    other = lax.ppermute(sums, "head", [(0, 1), (1, 0)])
    sums = sums.astype(F32) + other.astype(F32)
    concepts = dots.shape[0]
    saliency = scaled_scores(
        sums[:concepts, :img_rows], sums[:concepts, img_rows], sums[concepts, :img_rows], width
    )
    return (img_out, saliency)


def place(x, zl, y, c, g):
    return ((((x * 2 + zl) * 4 + y) * 2 + c) * 2) + g


def pairs(move):
    found = []
    for x in range(4):
        for zl in range(2):
            for y in range(4):
                for c in range(2):
                    for g in range(2):
                        found.append((place(x, zl, y, c, g), place(*move(x, zl, y, c, g))))
    return found


def along_z(s):
    def move(x, zl, y, c, g):
        z = (2 * g + zl + s) % 4
        return x, z % 2, y, c, z // 2

    return pairs(move)


def along_u(s):
    def move(x, zl, y, c, g):
        if c == 0:
            return (x + s) % 4, zl, y, c, g
        return x, zl, (y + s) % 4, c, g

    return pairs(move)


def along_v(s):
    def move(x, zl, y, c, g):
        if c == 0:
            return x, zl, (y + s) % 4, c, g
        return (x + s) % 4, zl, y, c, g

    return pairs(move)


def swap(dzl, dc, dg):
    return pairs(lambda x, zl, y, c, g: (x, zl ^ dzl, y, c ^ dc, g ^ dg))


def send(array, pairing):
    return lax.ppermute(array, ("ctx", "head"), pairing)


def nt(a, b, **kw):
    return lax.dot_general(a, b, (((1,), (1,)), ((), ())), preferred_element_type=F32, **kw)


def nn(a, b):
    return lax.dot_general(a, b, (((1,), (0,)), ((), ())), preferred_element_type=F32)


def call(kernel, outs, scratch=(), limit=48, flops=0, nbytes=0, smem=1):
    def run(*args):
        vm = pl.BlockSpec(memory_space=pltpu.VMEM)
        sm = pl.BlockSpec(memory_space=pltpu.SMEM)
        return pl.pallas_call(
            kernel,
            out_shape=outs,
            in_specs=[sm] * smem + [vm] * (len(args) - smem),
            out_specs=jax.tree.map(lambda _: vm, outs),
            scratch_shapes=list(scratch),
            compiler_params=pltpu.CompilerParams(vmem_limit_bytes=limit * MIB),
            cost_estimate=pl.CostEstimate(flops=flops, bytes_accessed=nbytes, transcendentals=0),
        )(*args)

    return run


def sds(shape, dtype=BF):
    return jax.ShapeDtypeStruct(shape, dtype)


def column_of(owner):
    ctx = owner >> 1
    return ((ctx >> 4) << 2) | ((ctx >> 1) & 3)


def ranks(keys, classes, resets):
    n = keys.shape[1]
    blk = 256
    row = lax.broadcasted_iota(jnp.int32, (blk, blk), 0)
    col = lax.broadcasted_iota(jnp.int32, (blk, blk), 1)
    earlier = (row < col).astype(F32).astype(BF)
    label = lax.broadcasted_iota(jnp.int32, (classes, blk), 0)
    carry = jnp.zeros((classes, 1), F32)
    found, peaks = [], []
    for b in range(n // blk):
        if b in resets:
            peaks.append(jnp.max(carry, axis=0, keepdims=True))
            carry = jnp.zeros((classes, 1), F32)
        hot = (label == keys[:, b * blk : (b + 1) * blk]).astype(F32)
        before = nn(hot.astype(BF), earlier) + carry
        found.append(jnp.sum(hot * before, axis=0, keepdims=True))
        carry = carry + jnp.sum(hot, axis=1, keepdims=True)
    peaks.append(jnp.max(carry, axis=0, keepdims=True))
    return jnp.concatenate(found, axis=1).astype(jnp.int32), peaks


def plan_kernel(at, ids_ref, table_ref, rows_ref, plan_ref):
    ids = ids_ref[...]
    n = ids.shape[1]
    vocab_dev = table_ref.shape[0]
    owner = ids >> int(math.log2(vocab_dev))
    rank, (most,) = ranks(owner, 128, ())
    hot_slot = lax.broadcasted_iota(jnp.int32, (SLOTS, n), 0) == rank
    hot_slot = (hot_slot & (owner == at[0])).astype(F32).astype(BF)
    hot_row = lax.broadcasted_iota(jnp.int32, (vocab_dev, n), 0) == (ids & (vocab_dev - 1))
    pick = nt(hot_slot, hot_row.astype(F32).astype(BF)).astype(BF)
    rows_ref[...] = nn(pick, table_ref[...]).astype(BF)
    spot, (con_most, txt_most) = ranks(column_of(owner), 16, (n * 2 // 3 // 256,))
    plan_ref[0:1, :] = rank
    plan_ref[1:2, :] = spot
    plan_ref[2:3, :] = jnp.broadcast_to(most.astype(jnp.int32), (1, n))
    plan_ref[3:4, :] = jnp.broadcast_to(con_most.astype(jnp.int32), (1, n))
    plan_ref[4:5, :] = jnp.broadcast_to(txt_most.astype(jnp.int32), (1, n))
    plan_ref[5:8, :] = jnp.zeros((3, n), jnp.int32)


def pack_kernel(at, ids_ref, plan_ref, out_ref):
    ids = ids_ref[...]
    n = ids.shape[1]
    owner = ids >> 8
    here = column_of(owner) == at[1]
    rank = plan_ref[0:1, :]
    spot = plan_ref[1:2, :]
    concept = lax.broadcasted_iota(jnp.int32, (1, n), 1) < (n * 2 // 3)
    target = jnp.where(
        concept, jnp.where(spot < CON, spot, -1), jnp.where(spot < TXT, spot + CON, -1)
    )
    z = ((owner & 1) << 1) | ((owner >> 4) & 1)
    core = (owner >> 1) & 1
    piece = jnp.where(core == at[2], 0, 4) + ((at[3] - z) & 3)
    source = jnp.where(rank < SLOTS, piece * SLOTS + rank, -1)
    target = jnp.where(here, target, -1)
    source = jnp.where(here, source, -1)
    hot_t = (lax.broadcasted_iota(jnp.int32, (ROWS, n), 0) == target).astype(F32).astype(BF)
    hot_s = (lax.broadcasted_iota(jnp.int32, (8 * SLOTS, n), 0) == source).astype(F32).astype(BF)
    out_ref[...] = nt(hot_t, hot_s).astype(BF)


def project_kernel(at, pack_ref, *refs):
    rows, (mod_ref, gain_ref, w_ref), outs, (x_ref,) = refs[:8], refs[8:11], refs[11:15], refs[15:]
    shift = mod_ref[0:1, :]
    scale = 1.0 + mod_ref[1:2, :]
    for i, ref in enumerate(rows):
        values = ref[...].astype(F32)
        mean = jnp.mean(values, axis=1, keepdims=True)
        centered = values - mean
        var = jnp.mean(centered * centered, axis=1, keepdims=True)
        x_ref[i * SLOTS : (i + 1) * SLOTS, :] = (
            centered * lax.rsqrt(var + 1e-06) * scale + shift
        ).astype(BF)
    x = nn(pack_ref[...], x_ref[...]).astype(BF)

    def normed(u, gain):
        meansq = jnp.mean(u * u, axis=1, keepdims=True)
        return u * lax.rsqrt(meansq + 1e-06) * gain

    q = nn(x[:CON], w_ref[0])
    k = nn(x, w_ref[1])
    v = nn(x, w_ref[2])
    heads = []
    for h in range(3):
        lanes = slice(h * HD, (h + 1) * HD)
        heads.append(
            (
                normed(q[:, lanes], gain_ref[0:1, :]).astype(BF),
                normed(k[:, lanes], gain_ref[1:2, :]).astype(BF),
                v[:, lanes].astype(BF),
            )
        )
    for s, out in enumerate(outs):
        head = (at[4] + s) & 3
        out[CON:, 0:HD] = jnp.zeros((TXT, HD), BF)
        for h in range(3):

            @pl.when(jnp.minimum(head, 2) == h)
            def _(h=h, out=out):
                out[0:CON, 0:HD] = heads[h][0]
                out[:, HD : 2 * HD] = heads[h][1]
                out[:, 2 * HD : 3 * HD] = heads[h][2]


def join_kernel(a, b, c, d, out):
    for i, ref in enumerate((a, b, c, d)):
        out[i * CON : (i + 1) * CON, :] = ref[0:CON, :]
        out[4 * CON + i * TXT : 4 * CON + (i + 1) * TXT, :] = ref[CON:, :]


def image_halves_kernel(at, q, kv, kvz, mine, theirs):
    half = q.shape[1] // 2
    n, m = q.shape[0], kv.shape[0]
    for out, core in ((mine, at[2]), (theirs, 1 - at[2])):
        lanes = pl.ds(pl.multiple_of(core * half, half), half)
        out[0:n, :] = q[:, lanes]
        out[n : n + m, :] = kv[:, lanes]
        out[n + m : n + 2 * m, :] = kvz[:, lanes]


def image_heads_kernel(at, mine, other, *outs):
    n = mine.shape[0]
    for s, out in enumerate(outs):
        head = jnp.minimum((at[4] + s) & 3, 2)
        lanes = pl.ds(pl.multiple_of(head * HD, HD), HD)
        out[0:n, :] = mine[:, lanes]
        out[n:, :] = other[:, lanes]


def image_join_kernel(a, b, c, d, q_out, kv_out):
    n = 32
    for i, ref in enumerate((a, b, c, d)):
        for j in range(2):
            base = j * 5 * n
            q_out[(2 * i + j) * n : (2 * i + j + 1) * n, :] = ref[base : base + n, :]
            for m in range(2):
                row = (4 * i + 2 * j + m) * n
                src = base + (1 + 2 * m) * n
                kv_out[row : row + n, :] = ref[src : src + n, :]
                kv_out[16 * n + row : 16 * n + row + n, :] = ref[src + n : src + 2 * n, :]


def attend(q, keys, values):
    scores = nt(q, keys)
    peak = jnp.max(scores, axis=1, keepdims=True)
    weights = jnp.exp2((scores - peak) * (HD ** (-0.5) * math.log2(math.e)))
    total = jnp.sum(weights, axis=1, keepdims=True)
    return (nn(weights.astype(BF), values) / total).astype(BF)


def attention_kernel(pc, pt, c0, c1, c2, c3, i0, i1, i2, i3, q, o0, o1, o2, o3, qc, keys, vals, co):
    chunks = (c0, c1, c2, c3)
    con = sum(
        nn(pc[:, a * 4 * CON : (a + 1) * 4 * CON], ref[0 : 4 * CON, :])
        for a, ref in enumerate(chunks)
    ).astype(BF)
    txt = sum(
        nn(pt[:, a * 4 * TXT : (a + 1) * 4 * TXT], ref[4 * CON :, HD:])
        for a, ref in enumerate(chunks)
    ).astype(BF)
    n_con, n_txt, n_img = con.shape[0], txt.shape[0], 4 * i0.shape[0] // 2
    qc[...] = con[:, 0:HD]
    keys[0:n_txt, :] = txt[:, 0:HD]
    vals[0:n_txt, :] = txt[:, HD:]
    part = n_img // 4
    for i, ref in enumerate((i0, i1, i2, i3)):
        row = n_txt + i * part
        keys[row : row + part, :] = ref[0:part, :]
        vals[row : row + part, :] = ref[part:, :]
    keys[n_txt + n_img :, :] = con[:, HD : 2 * HD]
    vals[n_txt + n_img :, :] = con[:, 2 * HD :]
    for b in range(n_con // 256):
        rows = slice(b * 256, (b + 1) * 256)
        co[rows, :] = attend(qc[rows, :], keys[n_txt:, :], vals[n_txt:, :])
    img = attend(q[...], keys[0 : n_txt + n_img, :], vals[0 : n_txt + n_img, :])
    con_out = co[...]
    dots = nt(img, con_out).astype(BF)
    con_f = con_out.astype(F32)
    con_sq = nt(jnp.ones((16, HD), F32), con_f * con_f, precision=lax.Precision.HIGHEST).astype(BF)
    for s, out in enumerate((o0, o1, o2, o3)):
        rows = slice(s * 64, (s + 1) * 64)
        out[0:64, 0:n_con] = dots[rows]
        out[0:64, n_con:] = img[rows]
        out[64:80, 0:n_con] = con_sq
        out[64:80, n_con:] = jnp.zeros((16, HD), BF)


def head_sum_kernel(at, b0, b1, b2, b3, own, core, diag, out_own):
    n_con = b0.shape[1] - HD
    total = jnp.zeros((80, n_con), F32)
    outs = [jnp.zeros((64, HD), BF) for _ in range(3)]
    for s, ref in enumerate((b0, b1, b2, b3)):
        head = (at[4] + s) & 3
        total = total + jnp.where(head < 3, ref[:, 0:n_con].astype(F32), 0.0)
        for h in range(3):
            outs[h] = jnp.where(head == h, ref[0:64, n_con:], outs[h])
    image_sq = jnp.zeros((64, 1), F32)
    for h in range(3):
        out_f = outs[h].astype(F32)
        image_sq = image_sq + jnp.sum(out_f * out_f, axis=1, keepdims=True)
    image_sq = jnp.broadcast_to(image_sq, (64, HD)).astype(BF)
    total = total.astype(BF)
    for ref, row in ((own, 0), (core, 32), (diag, 32)):
        ref[0:32, 0:n_con] = total[row : row + 32]
        ref[32:48, 0:n_con] = total[64:80]
        ref[0:32, n_con : n_con + HD] = image_sq[row : row + 32]
        ref[32:48, n_con : n_con + HD] = jnp.zeros((16, HD), BF)
    for h in range(3):
        lanes = slice(n_con + (1 + h) * HD, n_con + (2 + h) * HD)
        core[0:32, lanes] = outs[h][32:64]
        core[32:48, lanes] = jnp.zeros((16, HD), BF)
        out_own[:, h * HD : (h + 1) * HD] = outs[h][0:32]


def finish_kernel(at, own, core, head, diag, out_own, img_ref, sal_ref):
    n_con = own.shape[1] - HD
    width = 12 * HD
    cols = n_con + HD
    near = own[...].astype(F32) + core[:, 0:cols].astype(F32)
    far = head[...].astype(F32) + diag[...].astype(F32)
    total = near + far
    con_rms = jnp.sqrt(total[32:33, 0:n_con] / width + 1e-06)
    img_rms = jnp.sqrt(total[0:32, n_con : n_con + 1] / width + 1e-06)
    sal = total[0:32, 0:n_con] / (math.sqrt(width) * con_rms * img_rms)
    sal_ref[...] = jnp.transpose(sal)
    half = 3 * HD
    mine = pl.ds(pl.multiple_of(at[2] * half, half), half)
    theirs = pl.ds(pl.multiple_of((1 - at[2]) * half, half), half)
    img_ref[:, mine] = out_own[...]
    img_ref[:, theirs] = core[0:32, cols:]


def packed(
    img_q, img_k, img_v, txt_ids, concept_ids, step_index, token_table, modulation, txt_qkv, qk_gain
):
    n_con, n_txt = concept_ids.shape[0], txt_ids.shape[0]
    ctx = lax.axis_index("ctx")
    g = lax.axis_index("head")
    c = ctx & 1
    y = (ctx >> 1) & 3
    zl = (ctx >> 3) & 1
    x = ctx >> 4
    u = jnp.where(c == 0, x, y)
    v = jnp.where(c == 0, y, x)
    at = jnp.stack([ctx * 2 + g, x * 4 + y, c, 2 * g + zl, u, v]).astype(jnp.int32)
    ids = jnp.concatenate([concept_ids, txt_ids])[None, :]
    n = n_con + n_txt
    width = token_table.shape[1]

    kv = jnp.concatenate([img_k, img_v], axis=0)
    kvz = send(kv, swap(1, 0, 0))

    own_rows, plan = call(
        plan_kernel, (sds((SLOTS, width)), sds((8, n), jnp.int32)), nbytes=2 * MIB, flops=10**9
    )(at, ids, token_table)
    column_rows = [own_rows] + [send(own_rows, along_z(s)) for s in (1, 2, 3)]
    other_rows = [send(r, swap(0, 1, 0)) for r in column_rows]

    pack = call(pack_kernel, sds((ROWS, 8 * SLOTS)), nbytes=MIB, flops=10**9)(at, ids, plan)

    owner = ids[0] >> 8
    item_x = owner >> 5
    item_y = (owner >> 2) & 3
    item_u = jnp.where(c == 0, item_x, item_y)
    item_v = jnp.where(c == 0, item_y, item_x)
    block = ((v - item_v) & 3) * 4 + ((u - item_u) & 3)
    spot = plan[1]
    con_slot = block[:n_con] * CON + spot[:n_con]
    txt_slot = block[n_con:] * TXT + spot[n_con:]
    pick_con = (con_slot[:, None] == jnp.arange(16 * CON)[None, :]).astype(BF)
    pick_txt = (txt_slot[:, None] == jnp.arange(16 * TXT)[None, :]).astype(BF)

    half = txt_qkv.shape[2] // 2
    weights = lax.dynamic_slice_in_dim(jnp.transpose(txt_qkv, (1, 0, 2)), c * half, half, axis=2)
    shift_scale = lax.dynamic_index_in_dim(modulation, step_index[0], 0, keepdims=False)

    n_img = img_q.shape[0]
    mine, theirs = call(
        image_halves_kernel, (sds((5 * n_img, half)), sds((5 * n_img, half))), nbytes=MIB // 2
    )(at, img_q, kv, kvz)
    other = send(theirs, swap(0, 1, 0))
    image_blocks = call(
        image_heads_kernel, tuple(sds((10 * n_img, HD)) for _ in range(4)), nbytes=MIB // 2
    )(at, mine, other)
    image_blocks = [image_blocks[0]] + [send(image_blocks[s], along_u(s)) for s in (1, 2, 3)]
    image_q, image_kv = call(
        image_join_kernel, (sds((8 * n_img, HD)), sds((32 * n_img, HD))), nbytes=MIB // 2, smem=0
    )(*image_blocks)
    image_kvs = [image_kv] + [send(image_kv, along_v(s)) for s in (1, 2, 3)]

    qkv = call(
        project_kernel,
        tuple(sds((ROWS, 3 * HD)) for _ in range(4)),
        scratch=(pltpu.VMEM((8 * SLOTS, width), BF),),
        nbytes=10 * MIB,
        flops=10**9,
    )(at, pack, *column_rows, *other_rows, shift_scale, qk_gain, weights)
    qkv = [qkv[0]] + [send(qkv[s], along_u(s)) for s in (1, 2, 3)]
    joined = call(join_kernel, sds((4 * ROWS, 3 * HD)), nbytes=MIB, smem=0)(*qkv)
    chunks = [joined] + [send(joined, along_v(s)) for s in (1, 2, 3)]

    n_keys = n_txt + 64 * n_img + n_con
    blocks = call(
        attention_kernel,
        tuple(sds((80, n_con + HD)) for _ in range(4)),
        scratch=(
            pltpu.VMEM((n_con, HD), BF),
            pltpu.VMEM((n_keys, HD), BF),
            pltpu.VMEM((n_keys, HD), BF),
            pltpu.VMEM((n_con, HD), BF),
        ),
        nbytes=10 * MIB,
        flops=4 * 10**9,
        smem=0,
    )(pick_con, pick_txt, *chunks, *image_kvs, image_q)
    blocks = [blocks[0]] + [send(blocks[s], along_u(-s)) for s in (1, 2, 3)]
    own, core, diag, out_own = call(
        head_sum_kernel,
        (sds((48, n_con + HD)), sds((48, n_con + 4 * HD)), sds((48, n_con + HD)), sds((32, half))),
        nbytes=MIB,
    )(at, *blocks)
    from_head = send(own, swap(0, 0, 1))
    from_diag = send(diag, swap(0, 1, 1))
    from_core = send(core, swap(0, 1, 0))
    img_out, saliency = call(
        finish_kernel, (sds((n_img, 2 * half)), sds((n_con, n_img), F32)), nbytes=MIB
    )(at, own, from_core, from_head, from_diag, out_own)
    fits = (plan[2, 0] <= SLOTS) & (plan[3, 0] <= CON) & (plan[4, 0] <= TXT)
    return img_out, saliency, fits


def on_device(*args):
    img_out, saliency, fits = packed(*args)
    return lax.cond(fits, lambda: (img_out, saliency), lambda: general(*args))


def solution(mesh):
    return jax.shard_map(
        on_device,
        mesh=mesh,
        in_specs=(
            P("ctx", "head"),
            P("ctx", "head"),
            P("ctx", "head"),
            P(),
            P(),
            P(),
            P(("ctx", "head"), None),
            P(),
            P(None, None, "head"),
            P(),
        ),
        out_specs=(P("ctx", "head"), P(None, "ctx")),
        check_vma=False,
    )
```

time: 490 us -> 105 us (0.21)
  waiting for transfers between devices: 336 us -> 24.7 us
  local copies, waits for them, and re-layouts: 52.6 us -> 11.3 us
  Pallas kernels: 0 us -> 24.4 us
  matrix products: 24 us -> 0 us
  other arithmetic: 22.6 us -> 2.69 us
  between operations: 15 us -> 3.41 us
  starting transfers between devices: 27.6 us -> 38.1 us
  blocking collectives: 10 us -> 0 us
    all_to_all x3 -> x0, waiting for transfers between devices: 192 us -> none  [the longest x1 169 us: on_device(): lax.all_to_all(mine.reshape(n_all, -1, mine.shape[1]), ('ctx', 'head'), 0...]
    all_gather x2 -> x0, waiting for transfers between devices: 139 us -> none  [the longest x1 132 us: on_device(): lax.all_gather(img_v, 'ctx', axis=0, tiled=True)]
    ppermute x1 -> x27, starting transfers between devices: 1.74 us -> 38.1 us  [send(): return lax.ppermute(array, ('ctx', 'head'), pairing)]
    all_to_all x3 -> x0, starting transfers between devices: 25.8 us -> none  [the longest x2 13.9 us: gather_ctx(): return lax.all_to_all(spread, 'ctx', 0, 0, tiled=True)]
    pallas_call x0 -> x10, Pallas kernels: none -> 24.4 us  [run(): pl.pallas_call(kernel, out_shape=outs, in_specs=[sm] * smem + [vm] * (len...]
    dot_general x9 -> x0, matrix products: 24 us -> none  [the longest x1 6.98 us: on_device(): jnp.einsum('rd,dgc->rgc', concept_mod, txt_qkv, preferred_element_type=jn...]
    gather x2 -> x0, local copies, waits for them, and re-layouts: 21.9 us -> none  [on_device(): picked = jnp.take(token_table, jnp.clip(wanted, 0, vocab_dev - 1), axis=0)]
    ppermute x1 -> x27, waiting for transfers between devices: 3.88 us -> 24.7 us  [send(): return lax.ppermute(array, ('ctx', 'head'), pairing)]
  transfers between devices with their start and end apart: 6 -> 27, of which waited for: 5 -> 10; matrix products, arithmetic and copies ran while one was open for 7% -> 10% of each run, Pallas kernels for 0% -> 8%
where the time goes in v2:
time: 105 us
  starting transfers between devices  38.1 us (36%)
  waiting for transfers between devices  24.7 us (24%)
  Pallas kernels  24.4 us (23%)
  local copies, waits for them, and re-layouts  11.3 us (11%)
  between operations  3.41 us (3%)
  other arithmetic  2.69 us (3%)
    ppermute x27, starting transfers between devices, send(): return lax.ppermute(array, ('ctx', 'head'), pairing)  38.1 us
    ppermute x27, waiting for transfers between devices, send(): return lax.ppermute(array, ('ctx', 'head'), pairing)  24.7 us
    pallas_call x10, Pallas kernels, run(): pl.pallas_call(kernel, out_shape=outs, in_specs=[sm] * smem + [vm] * (len...  24.4 us
    dynamic_slice x1, local copies, waits for them, and re-layouts, packed(): lax.dynamic_slice_in_dim(jnp.transpose(txt_qkv, (1, 0, 2)), c * half, hal...  6.59 us
    convert_element_type x1, other arithmetic, packed(): pick_con = (con_slot[:, None] == jnp.arange(16 * CON)[None, :]).astype(BF)  2.44 us
  transfers between devices with their start and end apart: 27, of which 10 were waited for; matrix products, arithmetic and copies ran while one was open for 10% of the time, Pallas kernels for 8%

profile of v2, /device:TPU:1, one launch (start us, length us, event | category | flops | bytes accessed | tf_op | source)
XLA Modules:
  0.0 104.8 jit_solution(16359605845037993129)
XLA Ops:
  2.1 2.7 %shard_map.115 = (bf16[32,3072]{1,0:T(8,128)(2,1)S(1)}, s32[8,1536]{1,0:T(8,128)S(1)}) custom-call(s32[6]{0:T(128)S(1)} %stack.45.at, s32[1,1536]{1,0:T(1,128)S(1)} %broadcast_in_dim.36.ids_ref, bf16[256,3072]{1,0:T(8,128)(2,1)} %table_ref.1), custom_call_target="tpu_custom_call" | custom-call | flops 1000000000 | bytes 2097152 | tf_op jit(solution)/shard_map/pallas_call | solution.py:217
  4.9 2.5 %collective-permute-start.1 = (bf16[32,3072]{1,0:T(8,128)(2,1)S(1)}, bf16[32,3072]{1,0:T(8,128)(2,1)S(1)}, u32[]{:S(2)}, u32[]{:S(2)}) collective-permute-start(bf16[32,3072]{1,0:T(8,128)(2,1)S(1)} %get-tuple-element.59.refs_0_), channel_id=1, source_target_pairs={{0,16},{1,17},{2,18},{3,19},{4,20},{5,21},{6,22},{7,23},{8,24},{9,... | collective-permute-start | bytes 589832 | tf_op jit(solution)/shard_map/ppermute | solution.py:202
  7.4 3.3 %collective-permute-start.2 = (bf16[32,3072]{1,0:T(8,128)(2,1)S(1)}, bf16[32,3072]{1,0:T(8,128)(2,1)S(1)}, u32[]{:S(2)}, u32[]{:S(2)}) collective-permute-start(bf16[32,3072]{1,0:T(8,128)(2,1)S(1)} %get-tuple-element.59.refs_0_), channel_id=1, source_target_pairs={{0,1},{1,0},{2,3},{3,2},{4,5},{5,4},{6,7},{7,6},{8,9},{9,8},{10,11... | collective-permute-start | bytes 589832 | tf_op jit(solution)/shard_map/ppermute | solution.py:202
  11.5 1.5 %collective-permute-start.4 = (bf16[32,3072]{1,0:T(8,128)(2,1)S(1)}, bf16[32,3072]{1,0:T(8,128)(2,1)S(1)}, u32[]{:S(2)}, u32[]{:S(2)}) collective-permute-start(bf16[32,3072]{1,0:T(8,128)(2,1)S(1)} %get-tuple-element.59.refs_0_), channel_id=1, source_target_pairs={{0,2},{1,3},{2,0},{3,1},{4,6},{5,7},{6,4},{7,5},{8,10},{9,11},{10,... | collective-permute-start | bytes 589832 | tf_op jit(solution)/shard_map/ppermute | solution.py:202
  14.5 6.6 %dynamic-slice_bitcast_fusion.refs_10_ = bf16[3,3072,384]{2,1,0:T(8,128)(2,1)} fusion(bf16[3072,3,768]{2,0,1:T(8,128)(2,1)} %param.20, s32[]{:T(128)S(6)} %select_n.62), kind=kLoop, calls=%fused_computation.116 | loop fusion | bytes 14155780 | tf_op jit(solution)/shard_map/dynamic_slice | solution.py:514
  23.7 1.0 shard_map.116.pack_ref
  25.3 1.4 %collective-permute-start.16 = (bf16[320,128]{1,0:T(8,128)(2,1)S(1)}, bf16[320,128]{1,0:T(8,128)(2,1)S(1)}, u32[]{:S(2)}, u32[]{:S(2)}) collective-permute-start(bf16[320,128]{1,0:T(8,128)(2,1)S(1)} %get-tuple-element.67), channel_id=1, source_target_pairs={{0,32},{1,33},{2,6},{3,7},{4,36},{5,37},{6,10},{7,11},{8,40},{9,41... | collective-permute-start | bytes 245768 | tf_op jit(solution)/shard_map/ppermute | solution.py:202
  26.7 2.6 %collective-permute-start.17 = (bf16[320,128]{1,0:T(8,128)(2,1)S(1)}, bf16[320,128]{1,0:T(8,128)(2,1)S(1)}, u32[]{:S(2)}, u32[]{:S(2)}) collective-permute-start(bf16[320,128]{1,0:T(8,128)(2,1)S(1)} %get-tuple-element.68), channel_id=1, source_target_pairs={{0,64},{1,65},{2,10},{3,11},{4,68},{5,69},{6,14},{7,15},{8,72},{9,... | collective-permute-start | bytes 245768 | tf_op jit(solution)/shard_map/ppermute | solution.py:202
  29.3 1.1 %collective-permute-start.18 = (bf16[320,128]{1,0:T(8,128)(2,1)S(1)}, bf16[320,128]{1,0:T(8,128)(2,1)S(1)}, u32[]{:S(2)}, u32[]{:S(2)}) collective-permute-start(bf16[320,128]{1,0:T(8,128)(2,1)S(1)} %get-tuple-element.69), channel_id=1, source_target_pairs={{0,96},{1,97},{2,14},{3,15},{4,100},{5,101},{6,2},{7,3},{8,104},{9... | collective-permute-start | bytes 245768 | tf_op jit(solution)/shard_map/ppermute | solution.py:202
  30.4 6.0 %shard_map.117 = (bf16[176,384]{1,0:T(8,128)(2,1)S(1)}, bf16[176,384]{1,0:T(8,128)(2,1)S(1)}, bf16[176,384]{1,0:T(8,128)(2,1)S(1)}, bf16[176,384]{1,0:T(8,128)(2,1)S(1)}) custom-call(s32[6]{0:T(128)S(1)} %stack.45.at, bf16[176,256]{1,0:T(8,128)(2,1)S(1)} %shard_map.116.pack_ref, bf16[32,3072]{1,0:T(8,128)(2,1)S(1)} %get-tuple-element.59.refs_0_, ...), custom_call_target="tpu_custom_call" | custom-call | flops 1000000000 | bytes 10485760 | tf_op jit(solution)/shard_map/pallas_call | solution.py:217
  36.5 1.4 %collective-permute-start.8 = (bf16[176,384]{1,0:T(8,128)(2,1)S(1)}, bf16[176,384]{1,0:T(8,128)(2,1)S(1)}, u32[]{:S(2)}, u32[]{:S(2)}) collective-permute-start(bf16[176,384]{1,0:T(8,128)(2,1)S(1)} %get-tuple-element.61), channel_id=1, source_target_pairs={{0,32},{1,33},{2,6},{3,7},{4,36},{5,37},{6,10},{7,11},{8,40},{9,41... | collective-permute-start | bytes 405512 | tf_op jit(solution)/shard_map/ppermute | solution.py:202
  38.7 1.3 %collective-permute-start.19 = (bf16[1024,128]{1,0:T(8,128)(2,1)S(1)}, bf16[1024,128]{1,0:T(8,128)(2,1)S(1)}, u32[]{:S(2)}, u32[]{:S(2)}) collective-permute-start(bf16[1024,128]{1,0:T(8,128)(2,1)S(1)} %get-tuple-element.70.i0), channel_id=1, source_target_pairs={{0,4},{1,5},{2,34},{3,35},{4,8},{5,9},{6,38},{7,39},{8,12},{9,13},... | collective-permute-start | bytes 786440 | tf_op jit(solution)/shard_map/ppermute | solution.py:202
  40.3 1.3 %collective-permute-done.8.b = bf16[176,384]{1,0:T(8,128)(2,1)S(1)} collective-permute-done((bf16[176,384]{1,0:T(8,128)(2,1)S(1)}, bf16[176,384]{1,0:T(8,128)(2,1)S(1)}, u32[]{:S(2)}, u32[]{:S(2)}) %collective-permute-start.8) | collective-permute-done | bytes 135200 | tf_op jit(solution)/shard_map/ppermute | solution.py:202
  41.6 1.7 %collective-permute-done.9.c = bf16[176,384]{1,0:T(8,128)(2,1)S(1)} collective-permute-done((bf16[176,384]{1,0:T(8,128)(2,1)S(1)}, bf16[176,384]{1,0:T(8,128)(2,1)S(1)}, u32[]{:S(2)}, u32[]{:S(2)}) %collective-permute-start.9) | collective-permute-done | bytes 135200 | tf_op jit(solution)/shard_map/ppermute | solution.py:202
  43.4 1.3 %collective-permute-start.11 = (bf16[704,384]{1,0:T(8,128)(2,1)S(1)}, bf16[704,384]{1,0:T(8,128)(2,1)S(1)}, u32[]{:S(2)}, u32[]{:S(2)}) collective-permute-start(bf16[704,384]{1,0:T(8,128)(2,1)S(1)} %shard_map.118.c0), channel_id=1, source_target_pairs={{0,4},{1,5},{2,34},{3,35},{4,8},{5,9},{6,38},{7,39},{8,12},{9,13},... | collective-permute-start | bytes 1622024 | tf_op jit(solution)/shard_map/ppermute | solution.py:202
  44.7 2.7 %collective-permute-start.12 = (bf16[704,384]{1,0:T(8,128)(2,1)S(1)}, bf16[704,384]{1,0:T(8,128)(2,1)S(1)}, u32[]{:S(2)}, u32[]{:S(2)}) collective-permute-start(bf16[704,384]{1,0:T(8,128)(2,1)S(1)} %shard_map.118.c0), channel_id=1, source_target_pairs={{0,8},{1,9},{2,66},{3,67},{4,12},{5,13},{6,70},{7,71},{8,0},{9,1},... | collective-permute-start | bytes 1622024 | tf_op jit(solution)/shard_map/ppermute | solution.py:202
  48.3 2.4 %fusion.81.pc = bf16[1024,1792]{1,0:T(8,128)(2,1)} fusion(s32[1024]{0:T(1024)S(1)} %fusion.83), kind=kLoop, calls=%fused_computation.115 | loop fusion | flops 3670016 | bytes 3674112 | tf_op jit(solution)/shard_map/convert_element_type | solution.py:510
  51.1 2.6 %collective-permute-start.21 = (bf16[1024,128]{1,0:T(8,128)(2,1)S(1)}, bf16[1024,128]{1,0:T(8,128)(2,1)S(1)}, u32[]{:S(2)}, u32[]{:S(2)}) collective-permute-start(bf16[1024,128]{1,0:T(8,128)(2,1)S(1)} %get-tuple-element.70.i0), channel_id=1, source_target_pairs={{0,12},{1,13},{2,98},{3,99},{4,0},{5,1},{6,102},{7,103},{8,4},{9,5... | collective-permute-start | bytes 786440 | tf_op jit(solution)/shard_map/ppermute | solution.py:202
  54.0 9.1 %collective-permute-done.20.i2 = bf16[1024,128]{1,0:T(8,128)(2,1)S(1)} collective-permute-done((bf16[1024,128]{1,0:T(8,128)(2,1)S(1)}, bf16[1024,128]{1,0:T(8,128)(2,1)S(1)}, u32[]{:S(2)}, u32[]{:S(2)}) %collective-permute-start.20) | collective-permute-done | bytes 262176 | tf_op jit(solution)/shard_map/ppermute | solution.py:202
  63.0 2.4 %collective-permute-done.21.i3 = bf16[1024,128]{1,0:T(8,128)(2,1)S(1)} collective-permute-done((bf16[1024,128]{1,0:T(8,128)(2,1)S(1)}, bf16[1024,128]{1,0:T(8,128)(2,1)S(1)}, u32[]{:S(2)}, u32[]{:S(2)}) %collective-permute-start.21) | collective-permute-done | bytes 262176 | tf_op jit(solution)/shard_map/ppermute | solution.py:202
  65.5 10.9 %shard_map.122 = (bf16[80,1152]{1,0:T(8,128)(2,1)S(1)}, bf16[80,1152]{1,0:T(8,128)(2,1)S(1)}, bf16[80,1152]{1,0:T(8,128)(2,1)S(1)}, bf16[80,1152]{1,0:T(8,128)(2,1)S(1)}) custom-call(bf16[1024,1792]{1,0:T(8,128)(2,1)} %fusion.81.pc, bf16[512,1024]{1,0:T(8,128)(2,1)S(1)} %fusion.82.pt, bf16[704,384]{1,0:T(8,128)(2,1)S(1)} %shard_map.118.c0, ...), custom_call_target="tpu_custom_call" | custom-call | flops 4000000000 | bytes 10485760 | tf_op jit(solution)/shard_map/pallas_call | solution.py:217
  76.3 1.1 %collective-permute-start.22 = (bf16[80,1152]{1,0:T(8,128)(2,1)S(1)}, bf16[80,1152]{1,0:T(8,128)(2,1)S(1)}, u32[]{:S(2)}, u32[]{:S(2)}) collective-permute-start(bf16[80,1152]{1,0:T(8,128)(2,1)S(1)} %get-tuple-element.73), channel_id=1, source_target_pairs={{0,96},{1,97},{2,14},{3,15},{4,100},{5,101},{6,2},{7,3},{8,104},{9... | collective-permute-start | bytes 552968 | tf_op jit(solution)/shard_map/ppermute | solution.py:202
  77.5 1.2 %collective-permute-start.23 = (bf16[80,1152]{1,0:T(8,128)(2,1)S(1)}, bf16[80,1152]{1,0:T(8,128)(2,1)S(1)}, u32[]{:S(2)}, u32[]{:S(2)}) collective-permute-start(bf16[80,1152]{1,0:T(8,128)(2,1)S(1)} %get-tuple-element.74), channel_id=1, source_target_pairs={{0,64},{1,65},{2,10},{3,11},{4,68},{5,69},{6,14},{7,15},{8,72},{9,... | collective-permute-start | bytes 552968 | tf_op jit(solution)/shard_map/ppermute | solution.py:202
  78.8 2.0 %collective-permute-done.22.b1 = bf16[80,1152]{1,0:T(8,128)(2,1)S(1)} collective-permute-done((bf16[80,1152]{1,0:T(8,128)(2,1)S(1)}, bf16[80,1152]{1,0:T(8,128)(2,1)S(1)}, u32[]{:S(2)}, u32[]{:S(2)}) %collective-permute-start.22) | collective-permute-done | bytes 184352 | tf_op jit(solution)/shard_map/ppermute | solution.py:202
  80.7 2.7 %collective-permute-done.23.b2 = bf16[80,1152]{1,0:T(8,128)(2,1)S(1)} collective-permute-done((bf16[80,1152]{1,0:T(8,128)(2,1)S(1)}, bf16[80,1152]{1,0:T(8,128)(2,1)S(1)}, u32[]{:S(2)}, u32[]{:S(2)}) %collective-permute-start.23) | collective-permute-done | bytes 184352 | tf_op jit(solution)/shard_map/ppermute | solution.py:202
  83.5 1.9 %collective-permute-done.24.b3 = bf16[80,1152]{1,0:T(8,128)(2,1)S(1)} collective-permute-done((bf16[80,1152]{1,0:T(8,128)(2,1)S(1)}, bf16[80,1152]{1,0:T(8,128)(2,1)S(1)}, u32[]{:S(2)}, u32[]{:S(2)}) %collective-permute-start.24) | collective-permute-done | bytes 184352 | tf_op jit(solution)/shard_map/ppermute | solution.py:202
  86.2 5.8 %collective-permute-start.25 = (bf16[48,1536]{1,0:T(8,128)(2,1)S(1)}, bf16[48,1536]{1,0:T(8,128)(2,1)S(1)}, u32[]{:S(2)}, u32[]{:S(2)}) collective-permute-start(bf16[48,1536]{1,0:T(8,128)(2,1)S(1)} %get-tuple-element.77), channel_id=1, source_target_pairs={{0,2},{1,3},{2,0},{3,1},{4,6},{5,7},{6,4},{7,5},{8,10},{9,11},{10,... | collective-permute-start | bytes 442376 | tf_op jit(solution)/shard_map/ppermute | solution.py:202
  92.0 2.5 %collective-permute-start.26 = (bf16[48,1152]{1,0:T(8,128)(2,1)S(1)}, bf16[48,1152]{1,0:T(8,128)(2,1)S(1)}, u32[]{:S(2)}, u32[]{:S(2)}) collective-permute-start(bf16[48,1152]{1,0:T(8,128)(2,1)S(1)} %get-tuple-element.76.own), channel_id=1, source_target_pairs={{0,1},{1,0},{2,3},{3,2},{4,5},{5,4},{6,7},{7,6},{8,9},{9,8},{10,11... | collective-permute-start | bytes 331784 | tf_op jit(solution)/shard_map/ppermute | solution.py:202
  98.1 2.9 %collective-permute-done.27.diag = bf16[48,1152]{1,0:T(8,128)(2,1)S(1)} collective-permute-done((bf16[48,1152]{1,0:T(8,128)(2,1)S(1)}, bf16[48,1152]{1,0:T(8,128)(2,1)S(1)}, u32[]{:S(2)}, u32[]{:S(2)}) %collective-permute-start.27) | collective-permute-done | bytes 110624 | tf_op jit(solution)/shard_map/ppermute | solution.py:202
  101.0 1.7 %shard_map.124 = (bf16[32,768]{1,0:T(8,128)(2,1)}, f32[1024,32]{1,0:T(8,128)}) custom-call(s32[6]{0:T(128)S(1)} %stack.45.at, bf16[48,1152]{1,0:T(8,128)(2,1)S(1)} %get-tuple-element.76.own, bf16[48,1536]{1,0:T(8,128)(2,1)S(1)} %collective-permute-done.25.core, bf16[48,1152]{1,0:T(8,128)(2,1)S(1)} %collective-permute-done.26.head, ...), custom_call_target="tpu_custom_call" | custom-call | bytes 1048576 | tf_op jit(solution)/shard_map/pallas_call | solution.py:217
  102.7 2.2 %conditional.1 = (bf16[32,768]{1,0:T(8,128)(2,1)}, f32[1024,32]{0,1:T(8,128)}) conditional(s32[]{:T(128)} %bitcast.32, (s32[512]{0:T(512)S(1)}, s32[1024]{0:T(1024)S(1)}, bf16[256,3072]{1,0:T(8,128)(2,1)S(1)}, s32[1]{0:T(128)}, f32[28,2,3072]{2,1,0:T(2,128)}, /*index=5*/bf16[3072,3,768]{2,0,1:T(8,128)(2,1)}, f32[2,128]{1,0:T(2,128)S(1)}, ...), branch_computations={%region_0.15_spmd, %region_15.16_spmd} | conditional | flops 778344960 | bytes 257951312 | solution.py:574
  103.0 1.9 %copy.69 = f32[1024,32]{0,1:T(8,128)} copy(f32[1024,32]{1,0:T(8,128)} %get-tuple-element.90) | data formatting | bytes 262144 | tf_op jit(solution)/shard_map
  (64 shorter events, 11.7 us)
Async XLA Ops:
  0.6 12.3 %copy-start.2 = (bf16[32,768]{1,0:T(8,128)(2,1)S(1)}, bf16[32,768]{1,0:T(8,128)(2,1)}, u32[]{:S(2)}) copy-start(bf16[32,768]{1,0:T(8,128)(2,1)} %param.13) | copy-start | bytes 147460
  0.6 12.3 %copy-start.3 = (bf16[32,768]{1,0:T(8,128)(2,1)S(1)}, bf16[32,768]{1,0:T(8,128)(2,1)}, u32[]{:S(2)}) copy-start(bf16[32,768]{1,0:T(8,128)(2,1)} %param.14) | copy-start | bytes 147460
  4.9 18.2 %collective-permute-start.1 = (bf16[32,3072]{1,0:T(8,128)(2,1)S(1)}, bf16[32,3072]{1,0:T(8,128)(2,1)S(1)}, u32[]{:S(2)}, u32[]{:S(2)}) collective-permute-start(bf16[32,3072]{1,0:T(8,128)(2,1)S(1)} %get-tuple-element.59.refs_0_), channel_id=1, source_target_pairs={{0,16},{1,17},{2,18},{3,19},{4,20},{5,21},{6,22},{7,23},{8,24},{9,... | collective-permute-start | bytes 589832 | tf_op jit(solution)/shard_map/ppermute | solution.py:202
  7.4 15.7 %collective-permute-start.2 = (bf16[32,3072]{1,0:T(8,128)(2,1)S(1)}, bf16[32,3072]{1,0:T(8,128)(2,1)S(1)}, u32[]{:S(2)}, u32[]{:S(2)}) collective-permute-start(bf16[32,3072]{1,0:T(8,128)(2,1)S(1)} %get-tuple-element.59.refs_0_), channel_id=1, source_target_pairs={{0,1},{1,0},{2,3},{3,2},{4,5},{5,4},{6,7},{7,6},{8,9},{9,8},{10,11... | collective-permute-start | bytes 589832 | tf_op jit(solution)/shard_map/ppermute | solution.py:202
  10.7 12.8 %collective-permute-start.3 = (bf16[32,3072]{1,0:T(8,128)(2,1)S(1)}, bf16[32,3072]{1,0:T(8,128)(2,1)S(1)}, u32[]{:S(2)}, u32[]{:S(2)}) collective-permute-start(bf16[32,3072]{1,0:T(8,128)(2,1)S(1)} %get-tuple-element.59.refs_0_), channel_id=1, source_target_pairs={{0,17},{1,16},{2,19},{3,18},{4,21},{5,20},{6,23},{7,22},{8,25},{9,... | collective-permute-start | bytes 589832 | tf_op jit(solution)/shard_map/ppermute | solution.py:202
  11.5 15.2 %collective-permute-start.4 = (bf16[32,3072]{1,0:T(8,128)(2,1)S(1)}, bf16[32,3072]{1,0:T(8,128)(2,1)S(1)}, u32[]{:S(2)}, u32[]{:S(2)}) collective-permute-start(bf16[32,3072]{1,0:T(8,128)(2,1)S(1)} %get-tuple-element.59.refs_0_), channel_id=1, source_target_pairs={{0,2},{1,3},{2,0},{3,1},{4,6},{5,7},{6,4},{7,5},{8,10},{9,11},{10,... | collective-permute-start | bytes 589832 | tf_op jit(solution)/shard_map/ppermute | solution.py:202
  13.0 8.8 %collective-permute-start.14 = (bf16[64,768]{1,0:T(8,128)(2,1)S(1)}, bf16[64,768]{1,0:T(8,128)(2,1)S(1)}, u32[]{:S(2)}, u32[]{:S(2)}) collective-permute-start(bf16[64,768]{1,0:T(8,128)(2,1)S(1)} %constant_dynamic-update-slice_fusion.1.kv), channel_id=1, source_target_pairs={{0,16},{1,17},{2,18},{3,19},{4,20},{5,21},{6,22},{7,23},{8,24},{9,... | collective-permute-start | bytes 294920 | tf_op jit(solution)/shard_map/ppermute | solution.py:202
  22.4 2.3 %collective-permute-start.15 = (bf16[160,384]{1,0:T(8,128)(2,1)S(1)}, bf16[160,384]{1,0:T(8,128)(2,1)S(1)}, u32[]{:S(2)}, u32[]{:S(2)}) collective-permute-start(bf16[160,384]{1,0:T(8,128)(2,1)S(1)} %get-tuple-element.65), channel_id=1, source_target_pairs={{0,2},{1,3},{2,0},{3,1},{4,6},{5,7},{6,4},{7,5},{8,10},{9,11},{10,... | collective-permute-start | bytes 368648 | tf_op jit(solution)/shard_map/ppermute | solution.py:202
  23.0 6.2 %collective-permute-start.5 = (bf16[32,3072]{1,0:T(8,128)(2,1)S(1)}, bf16[32,3072]{1,0:T(8,128)(2,1)S(1)}, u32[]{:S(2)}, u32[]{:S(2)}) collective-permute-start(bf16[32,3072]{1,0:T(8,128)(2,1)S(1)} %collective-permute-done.1.refs_1_), channel_id=1, source_target_pairs={{0,2},{1,3},{2,0},{3,1},{4,6},{5,7},{6,4},{7,5},{8,10},{9,11},{10,... | collective-permute-start | bytes 589832 | tf_op jit(solution)/shard_map/ppermute | solution.py:202
  23.2 7.2 %collective-permute-start.6 = (bf16[32,3072]{1,0:T(8,128)(2,1)S(1)}, bf16[32,3072]{1,0:T(8,128)(2,1)S(1)}, u32[]{:S(2)}, u32[]{:S(2)}) collective-permute-start(bf16[32,3072]{1,0:T(8,128)(2,1)S(1)} %collective-permute-done.2.refs_2_), channel_id=1, source_target_pairs={{0,2},{1,3},{2,0},{3,1},{4,6},{5,7},{6,4},{7,5},{8,10},{9,11},{10,... | collective-permute-start | bytes 589832 | tf_op jit(solution)/shard_map/ppermute | solution.py:202
  23.6 6.8 %collective-permute-start.7 = (bf16[32,3072]{1,0:T(8,128)(2,1)S(1)}, bf16[32,3072]{1,0:T(8,128)(2,1)S(1)}, u32[]{:S(2)}, u32[]{:S(2)}) collective-permute-start(bf16[32,3072]{1,0:T(8,128)(2,1)S(1)} %collective-permute-done.3.refs_3_), channel_id=1, source_target_pairs={{0,2},{1,3},{2,0},{3,1},{4,6},{5,7},{6,4},{7,5},{8,10},{9,11},{10,... | collective-permute-start | bytes 589832 | tf_op jit(solution)/shard_map/ppermute | solution.py:202
  25.3 12.7 %collective-permute-start.16 = (bf16[320,128]{1,0:T(8,128)(2,1)S(1)}, bf16[320,128]{1,0:T(8,128)(2,1)S(1)}, u32[]{:S(2)}, u32[]{:S(2)}) collective-permute-start(bf16[320,128]{1,0:T(8,128)(2,1)S(1)} %get-tuple-element.67), channel_id=1, source_target_pairs={{0,32},{1,33},{2,6},{3,7},{4,36},{5,37},{6,10},{7,11},{8,40},{9,41... | collective-permute-start | bytes 245768 | tf_op jit(solution)/shard_map/ppermute | solution.py:202
  26.7 12.0 %collective-permute-start.17 = (bf16[320,128]{1,0:T(8,128)(2,1)S(1)}, bf16[320,128]{1,0:T(8,128)(2,1)S(1)}, u32[]{:S(2)}, u32[]{:S(2)}) collective-permute-start(bf16[320,128]{1,0:T(8,128)(2,1)S(1)} %get-tuple-element.68), channel_id=1, source_target_pairs={{0,64},{1,65},{2,10},{3,11},{4,68},{5,69},{6,14},{7,15},{8,72},{9,... | collective-permute-start | bytes 245768 | tf_op jit(solution)/shard_map/ppermute | solution.py:202
  29.3 9.4 %collective-permute-start.18 = (bf16[320,128]{1,0:T(8,128)(2,1)S(1)}, bf16[320,128]{1,0:T(8,128)(2,1)S(1)}, u32[]{:S(2)}, u32[]{:S(2)}) collective-permute-start(bf16[320,128]{1,0:T(8,128)(2,1)S(1)} %get-tuple-element.69), channel_id=1, source_target_pairs={{0,96},{1,97},{2,14},{3,15},{4,100},{5,101},{6,2},{7,3},{8,104},{9... | collective-permute-start | bytes 245768 | tf_op jit(solution)/shard_map/ppermute | solution.py:202
  36.4 3.9 %collective-permute-start.10 = (bf16[176,384]{1,0:T(8,128)(2,1)S(1)}, bf16[176,384]{1,0:T(8,128)(2,1)S(1)}, u32[]{:S(2)}, u32[]{:S(2)}) collective-permute-start(bf16[176,384]{1,0:T(8,128)(2,1)S(1)} %get-tuple-element.63), channel_id=1, source_target_pairs={{0,96},{1,97},{2,14},{3,15},{4,100},{5,101},{6,2},{7,3},{8,104},{9... | collective-permute-start | bytes 405512 | tf_op jit(solution)/shard_map/ppermute | solution.py:202
  36.5 5.1 %collective-permute-start.8 = (bf16[176,384]{1,0:T(8,128)(2,1)S(1)}, bf16[176,384]{1,0:T(8,128)(2,1)S(1)}, u32[]{:S(2)}, u32[]{:S(2)}) collective-permute-start(bf16[176,384]{1,0:T(8,128)(2,1)S(1)} %get-tuple-element.61), channel_id=1, source_target_pairs={{0,32},{1,33},{2,6},{3,7},{4,36},{5,37},{6,10},{7,11},{8,40},{9,41... | collective-permute-start | bytes 405512 | tf_op jit(solution)/shard_map/ppermute | solution.py:202
  38.0 5.4 %collective-permute-start.9 = (bf16[176,384]{1,0:T(8,128)(2,1)S(1)}, bf16[176,384]{1,0:T(8,128)(2,1)S(1)}, u32[]{:S(2)}, u32[]{:S(2)}) collective-permute-start(bf16[176,384]{1,0:T(8,128)(2,1)S(1)} %get-tuple-element.62), channel_id=1, source_target_pairs={{0,64},{1,65},{2,10},{3,11},{4,68},{5,69},{6,14},{7,15},{8,72},{9,... | collective-permute-start | bytes 405512 | tf_op jit(solution)/shard_map/ppermute | solution.py:202
  38.7 12.4 %collective-permute-start.19 = (bf16[1024,128]{1,0:T(8,128)(2,1)S(1)}, bf16[1024,128]{1,0:T(8,128)(2,1)S(1)}, u32[]{:S(2)}, u32[]{:S(2)}) collective-permute-start(bf16[1024,128]{1,0:T(8,128)(2,1)S(1)} %get-tuple-element.70.i0), channel_id=1, source_target_pairs={{0,4},{1,5},{2,34},{3,35},{4,8},{5,9},{6,38},{7,39},{8,12},{9,13},... | collective-permute-start | bytes 786440 | tf_op jit(solution)/shard_map/ppermute | solution.py:202
  43.4 22.0 %collective-permute-start.11 = (bf16[704,384]{1,0:T(8,128)(2,1)S(1)}, bf16[704,384]{1,0:T(8,128)(2,1)S(1)}, u32[]{:S(2)}, u32[]{:S(2)}) collective-permute-start(bf16[704,384]{1,0:T(8,128)(2,1)S(1)} %shard_map.118.c0), channel_id=1, source_target_pairs={{0,4},{1,5},{2,34},{3,35},{4,8},{5,9},{6,38},{7,39},{8,12},{9,13},... | collective-permute-start | bytes 1622024 | tf_op jit(solution)/shard_map/ppermute | solution.py:202
  44.7 20.8 %collective-permute-start.12 = (bf16[704,384]{1,0:T(8,128)(2,1)S(1)}, bf16[704,384]{1,0:T(8,128)(2,1)S(1)}, u32[]{:S(2)}, u32[]{:S(2)}) collective-permute-start(bf16[704,384]{1,0:T(8,128)(2,1)S(1)} %shard_map.118.c0), channel_id=1, source_target_pairs={{0,8},{1,9},{2,66},{3,67},{4,12},{5,13},{6,70},{7,71},{8,0},{9,1},... | collective-permute-start | bytes 1622024 | tf_op jit(solution)/shard_map/ppermute | solution.py:202
  47.4 18.0 %collective-permute-start.13 = (bf16[704,384]{1,0:T(8,128)(2,1)S(1)}, bf16[704,384]{1,0:T(8,128)(2,1)S(1)}, u32[]{:S(2)}, u32[]{:S(2)}) collective-permute-start(bf16[704,384]{1,0:T(8,128)(2,1)S(1)} %shard_map.118.c0), channel_id=1, source_target_pairs={{0,12},{1,13},{2,98},{3,99},{4,0},{5,1},{6,102},{7,103},{8,4},{9,5... | collective-permute-start | bytes 1622024 | tf_op jit(solution)/shard_map/ppermute | solution.py:202
  50.7 12.3 %collective-permute-start.20 = (bf16[1024,128]{1,0:T(8,128)(2,1)S(1)}, bf16[1024,128]{1,0:T(8,128)(2,1)S(1)}, u32[]{:S(2)}, u32[]{:S(2)}) collective-permute-start(bf16[1024,128]{1,0:T(8,128)(2,1)S(1)} %get-tuple-element.70.i0), channel_id=1, source_target_pairs={{0,8},{1,9},{2,66},{3,67},{4,12},{5,13},{6,70},{7,71},{8,0},{9,1},... | collective-permute-start | bytes 786440 | tf_op jit(solution)/shard_map/ppermute | solution.py:202
  51.1 14.3 %collective-permute-start.21 = (bf16[1024,128]{1,0:T(8,128)(2,1)S(1)}, bf16[1024,128]{1,0:T(8,128)(2,1)S(1)}, u32[]{:S(2)}, u32[]{:S(2)}) collective-permute-start(bf16[1024,128]{1,0:T(8,128)(2,1)S(1)} %get-tuple-element.70.i0), channel_id=1, source_target_pairs={{0,12},{1,13},{2,98},{3,99},{4,0},{5,1},{6,102},{7,103},{8,4},{9,5... | collective-permute-start | bytes 786440 | tf_op jit(solution)/shard_map/ppermute | solution.py:202
  65.4 37.2 %copy-start = (bf16[256,3072]{1,0:T(8,128)(2,1)S(1)}, bf16[256,3072]{1,0:T(8,128)(2,1)}, u32[]{:S(2)}) copy-start(bf16[256,3072]{1,0:T(8,128)(2,1)} %table_ref.1) | copy-start | bytes 4718596
  65.4 37.2 %copy-start.8 = (s32[1024]{0:T(1024)S(1)}, s32[1024]{0:T(1024)}, u32[]{:S(2)}) copy-start(s32[1024]{0:T(1024)} %param.16) | copy-start | bytes 12292
  65.5 37.2 %copy-start.9 = (s32[512]{0:T(512)S(1)}, s32[512]{0:T(512)}, u32[]{:S(2)}) copy-start(s32[512]{0:T(512)} %param.15) | copy-start | bytes 6148
  76.3 4.4 %collective-permute-start.22 = (bf16[80,1152]{1,0:T(8,128)(2,1)S(1)}, bf16[80,1152]{1,0:T(8,128)(2,1)S(1)}, u32[]{:S(2)}, u32[]{:S(2)}) collective-permute-start(bf16[80,1152]{1,0:T(8,128)(2,1)S(1)} %get-tuple-element.73), channel_id=1, source_target_pairs={{0,96},{1,97},{2,14},{3,15},{4,100},{5,101},{6,2},{7,3},{8,104},{9... | collective-permute-start | bytes 552968 | tf_op jit(solution)/shard_map/ppermute | solution.py:202
  77.5 6.0 %collective-permute-start.23 = (bf16[80,1152]{1,0:T(8,128)(2,1)S(1)}, bf16[80,1152]{1,0:T(8,128)(2,1)S(1)}, u32[]{:S(2)}, u32[]{:S(2)}) collective-permute-start(bf16[80,1152]{1,0:T(8,128)(2,1)S(1)} %get-tuple-element.74), channel_id=1, source_target_pairs={{0,64},{1,65},{2,10},{3,11},{4,68},{5,69},{6,14},{7,15},{8,72},{9,... | collective-permute-start | bytes 552968 | tf_op jit(solution)/shard_map/ppermute | solution.py:202
  78.6 6.7 %collective-permute-start.24 = (bf16[80,1152]{1,0:T(8,128)(2,1)S(1)}, bf16[80,1152]{1,0:T(8,128)(2,1)S(1)}, u32[]{:S(2)}, u32[]{:S(2)}) collective-permute-start(bf16[80,1152]{1,0:T(8,128)(2,1)S(1)} %get-tuple-element.75), channel_id=1, source_target_pairs={{0,32},{1,33},{2,6},{3,7},{4,36},{5,37},{6,10},{7,11},{8,40},{9,41... | collective-permute-start | bytes 552968 | tf_op jit(solution)/shard_map/ppermute | solution.py:202
  86.2 14.8 %collective-permute-start.25 = (bf16[48,1536]{1,0:T(8,128)(2,1)S(1)}, bf16[48,1536]{1,0:T(8,128)(2,1)S(1)}, u32[]{:S(2)}, u32[]{:S(2)}) collective-permute-start(bf16[48,1536]{1,0:T(8,128)(2,1)S(1)} %get-tuple-element.77), channel_id=1, source_target_pairs={{0,2},{1,3},{2,0},{3,1},{4,6},{5,7},{6,4},{7,5},{8,10},{9,11},{10,... | collective-permute-start | bytes 442376 | tf_op jit(solution)/shard_map/ppermute | solution.py:202
  92.0 6.1 %collective-permute-start.26 = (bf16[48,1152]{1,0:T(8,128)(2,1)S(1)}, bf16[48,1152]{1,0:T(8,128)(2,1)S(1)}, u32[]{:S(2)}, u32[]{:S(2)}) collective-permute-start(bf16[48,1152]{1,0:T(8,128)(2,1)S(1)} %get-tuple-element.76.own), channel_id=1, source_target_pairs={{0,1},{1,0},{2,3},{3,2},{4,5},{5,4},{6,7},{7,6},{8,9},{9,8},{10,11... | collective-permute-start | bytes 331784 | tf_op jit(solution)/shard_map/ppermute | solution.py:202
  94.4 6.5 %collective-permute-start.27 = (bf16[48,1152]{1,0:T(8,128)(2,1)S(1)}, bf16[48,1152]{1,0:T(8,128)(2,1)S(1)}, u32[]{:S(2)}, u32[]{:S(2)}) collective-permute-start(bf16[48,1152]{1,0:T(8,128)(2,1)S(1)} %get-tuple-element.78), channel_id=1, source_target_pairs={{0,3},{1,2},{2,1},{3,0},{4,7},{5,6},{6,5},{7,4},{8,11},{9,10},{10,... | collective-permute-start | bytes 331784 | tf_op jit(solution)/shard_map/ppermute | solution.py:202
  (2 other events, 16.7 us)
